TPU v7x, 32 devices: a whole 2x2x4 slice. The times are simulated.
32 devices in a mesh: runs: 2 (over x), tile: 16 (over z, y, core).
Axes of the slice: x: 2, y: 2, z: 4, core: 2. Of those that a mesh axis runs over, the one named last changes fastest.
Arguments:
- fluid_press: float32 [8192, 128], P(('runs', 'tile')), parts along dimension 0, may hold values from -6 to 6
- iterate: float32 [8192, 128], P(('runs', 'tile')), parts along dimension 0, may hold values from -6 to 6
- displace: float32 [4096, 128], P(('runs', 'tile')), parts along dimension 0, may hold values from -6 to 6
- velocity: float32 [4096, 128], P(('runs', 'tile')), parts along dimension 0, may hold values from -6 to 6
- stiffness: float32 [4096, 128], P(('runs', 'tile')), parts along dimension 0, may hold values from 0.08 to 0.45
- owners: int32 [4096, 1], P(('runs', 'tile')), parts along dimension 0, may hold values from 0 to 15; in each aligned block of 128 rows (0 to 127, 128 to 255, ...) at most 16 rows name the same one
- diff_cur: bfloat16 [40, 8192, 128], P(None, ('runs', 'tile')), parts along dimension 1, may hold values from -1.1048543 to 1.1048543
- step_cur: bfloat16 [40, 8192, 128], P(None, ('runs', 'tile')), parts along dimension 1, may hold values from -6 to 6
- diff_past: bfloat16 [30, 8192, 128], P(None, ('runs', 'tile')), parts along dimension 1, may hold values from -1.1048543 to 1.1048543
- step_past: bfloat16 [30, 8192, 128], P(None, ('runs', 'tile')), parts along dimension 1, may hold values from -6 to 6
Outputs:
- new_iterate: float32 [8192, 128], P(('runs', 'tile')), parts along dimension 0
- displace_out: float32 [4096, 128], P(('runs', 'tile')), parts along dimension 0
- velocity_out: float32 [4096, 128], P(('runs', 'tile')), parts along dimension 0
There are 2 independent parts, one for each index of `runs`. A program takes and returns all parts, laid end to end along the dimension named above; each array names one. Nothing has to cross between parts.
Inputs may be any that keep to these rules, and one draw needn't show every extreme that they name: `owners`: in the 128 lines of one device no partition is named more than 16 times; some partition is named exactly 16 times.
All inputs are finite; a program needn't handle non-finite values.
Results may differ from a plain program's by a relative error of at most 0.0042.
Values sent between devices are 32-bit elements; how exact they have to be, the bound alone decides.
A program may use at most 64 MiB of HBM per device.

v0:
```python
import jax
import jax.numpy as jnp
from jax import lax
from jax.sharding import PartitionSpec as P

SUBSTEPS = 4


step_dt = 1.0
damping = 0.05


def padded_2(cells, sides, width):
    for axis, dim in sides:
        count = lax.axis_size(axis)
        head = lax.slice_in_dim(cells, 0, width, axis=dim)
        tail = lax.slice_in_dim(cells, cells.shape[dim] - width, cells.shape[dim], axis=dim)
        cells = jnp.concatenate(
            [
                lax.ppermute(tail, axis, [(i, (i + 1) % count) for i in range(count)]),
                cells,
                lax.ppermute(head, axis, [((i + 1) % count, i) for i in range(count)]),
            ],
            axis=dim,
        )
    return cells


def sides(center):
    zero_col = jnp.zeros((center.shape[0], 1), jnp.float32)
    left = jnp.concatenate([zero_col, center[:, :-1]], 1)
    right = jnp.concatenate([center[:, 1:], zero_col], 1)
    return left + right


def solve_spd(matrix, vector):
    factor = jnp.linalg.cholesky(matrix)
    inner = lax.linalg.triangular_solve(factor, vector[:, None], left_side=True, lower=True)
    outer = lax.linalg.triangular_solve(factor, inner, left_side=True, lower=True, transpose_a=True)
    return outer[:, 0]


def local(
    fluid_press,
    iterate,
    displace,
    velocity,
    stiffness,
    owners,
    diff_cur,
    step_cur,
    diff_past,
    step_past,
):
    high = lax.Precision.HIGHEST
    tile_count = lax.axis_size("tile")
    line_count = displace.shape[0]
    slot_count = iterate.shape[0]
    per_pair = slot_count // tile_count
    owner_list = owners[:, 0]
    onehot = (owner_list[:, None] == jnp.arange(tile_count, dtype=jnp.int32)[None, :]).astype(
        jnp.float32
    )
    below = (jnp.arange(line_count)[:, None] > jnp.arange(line_count)[None, :]).astype(jnp.float32)
    earlier = jnp.dot(below, onehot, precision=high)
    rank_in = jnp.sum(earlier * onehot, axis=1).astype(jnp.int32)
    slot_of = owner_list * per_pair + rank_in
    chooser = (slot_of[:, None] == jnp.arange(slot_count, dtype=jnp.int32)[None, :]).astype(
        jnp.float32
    )
    returned = lax.all_to_all(fluid_press, "tile", split_axis=0, concat_axis=0, tiled=True)
    pressure = jnp.dot(chooser, returned, precision=high)
    field, speed = (displace, velocity)
    for substep in range(SUBSTEPS):
        padded = padded_2(field, (("tile", 0),), 1)
        lapl = padded[:-2] + padded[2:] + sides(field) - 4.0 * field
        speed = speed + step_dt * (stiffness * lapl + pressure - damping * speed)
        field = field + step_dt * speed
    outgoing = jnp.dot(chooser.T, field, precision=high)
    flags = jnp.sum(chooser, axis=0)
    x_tilde, mask = (
        lax.all_to_all(outgoing, "tile", split_axis=0, concat_axis=0, tiled=True),
        lax.all_to_all(flags, "tile", split_axis=0, concat_axis=0, tiled=True),
    )
    mask_half = mask.astype(jnp.bfloat16)
    cur_cols = (diff_cur * mask_half[None, :, None]).reshape(diff_cur.shape[0], -1)
    past_cols = (diff_past * mask_half[None, :, None]).reshape(diff_past.shape[0], -1)
    resid = (mask[:, None] * (x_tilde - iterate)).astype(jnp.bfloat16).reshape(-1)
    gram_cur = lax.dot_general(
        cur_cols, cur_cols, (((1,), (1,)), ((), ())), preferred_element_type=jnp.float32
    )
    rhs_cur = jnp.dot(cur_cols, resid, preferred_element_type=jnp.float32)
    gram_past = lax.dot_general(
        past_cols, past_cols, (((1,), (1,)), ((), ())), preferred_element_type=jnp.float32
    )
    gram_cur, rhs_cur, gram_past = lax.psum((gram_cur, rhs_cur, gram_past), "tile")
    coeff = -solve_spd(gram_cur, rhs_cur)
    proj = resid.astype(jnp.float32) + jnp.dot(
        coeff, cur_cols, precision=high, preferred_element_type=jnp.float32
    )
    projected = lax.psum(
        jnp.dot(past_cols, proj, precision=high, preferred_element_type=jnp.float32), "tile"
    )
    past = solve_spd(gram_past, projected)
    upd_cur = jnp.dot(
        coeff.astype(jnp.bfloat16),
        step_cur.reshape(step_cur.shape[0], -1),
        preferred_element_type=jnp.float32,
    )
    upd_past = jnp.dot(
        past.astype(jnp.bfloat16),
        step_past.reshape(step_past.shape[0], -1),
        preferred_element_type=jnp.float32,
    )
    update = (upd_cur - upd_past).reshape(x_tilde.shape)
    new_iterate = mask[:, None] * (x_tilde + update)
    return (new_iterate, field, speed)


def solution(mesh):
    placed = (
        P(("runs", "tile"), None),
        P(("runs", "tile"), None),
        P(("runs", "tile"), None),
        P(("runs", "tile"), None),
        P(("runs", "tile"), None),
        P(("runs", "tile"), None),
        P(None, ("runs", "tile"), None),
        P(None, ("runs", "tile"), None),
        P(None, ("runs", "tile"), None),
        P(None, ("runs", "tile"), None),
    )
    return jax.shard_map(
        local,
        mesh=mesh,
        in_specs=placed,
        out_specs=(P(("runs", "tile"), None), P(("runs", "tile"), None), P(("runs", "tile"), None)),
        check_vma=False,
    )
```

profile of v0, /device:TPU:0, one launch (start us, length us, event | category | flops | bytes accessed | tf_op | source)
XLA Modules:
  0.0 210.5 jit_solution(13058534543472758253)
XLA Ops:
  0.6 0.7 fusion.90
  1.3 0.5 collective-permute-start
  1.8 5.0 %collective-permute-start.1 = (f32[1,128]{1,0:T(1,128)S(1)}, f32[1,128]{1,0:T(1,128)S(1)}, u32[]{:S(2)}, u32[]{:S(2)}) collective-permute-start(f32[1,128]{1,0:T(1,128)S(1)} %get-tuple-element.28), channel_id=1, source_target_pairs={{1,0},{2,1},{3,2},{4,3},{5,4},{6,5},{7,6},{8,7},{9,8},{10,9},{11,1... | collective-permute-start | bytes 1544 | tf_op jit(solution)/shard_map/ppermute | solution.py:22
  6.8 0.9 fusion.18
  7.7 0.7 fusion.74
  8.3 0.1 convert_reduce_fusion
  8.4 0.7 all_to_all.22
  9.1 3.7 %all-to-all-start = ((f32[16,16,1]{1,2,0:T(1,128)}), f32[16,16,1]{1,2,0:T(1,128)S(1)}, u32[]{:S(2)}, u32[]{:S(2)}) async-start(f32[16,16,1]{1,2,0:T(1,128)} %bitcast.3), calls=%async_computation | async-start | bytes 16384 | tf_op jit(solution)/shard_map/all_to_all | solution.py:83
  12.8 1.0 fusion.91
  13.8 1.8 pad.41
  15.6 2.7 %copy.55 = bf16[4,8,256,128]{3,1,2,0:T(8,128)(2,1)} copy(bf16[4,8,256,128]{3,2,1,0:T(8,128)(2,1)S(1)} %bitcast.116) | data formatting | bytes 4194304
  18.3 0.9 all-to-all-done
  19.2 5.2 %all-to-all-start.1 = ((f32[16,16,128]{2,1,0:T(8,128)}), f32[16,16,128]{2,1,0:T(8,128)S(1)}, u32[]{:S(2)}, u32[]{:S(2)}) async-start(f32[16,16,128]{2,1,0:T(8,128)} %bitcast.4), calls=%async_computation.1 | async-start | bytes 262144 | tf_op jit(solution)/shard_map/all_to_all | solution.py:71
  24.3 0.5 broadcast.160
  24.8 0.7 reduce.15
  25.5 0.1 mul.81
  25.6 2.1 %broadcast_multiply_fusion = bf16[40,256,128]{2,1,0:T(8,128)(2,1)S(1)} fusion(bf16[40,256,128]{2,1,0:T(8,128)(2,1)} %param.16, bf16[256]{0:T(256)(128)(2,1)S(1)} %convert_element_type.45), kind=kLoop, calls=%fused_computation.12 | loop fusion | flops 1310720 | bytes 5243392 | tf_op jit(solution)/shard_map/mul | solution.py:86
  27.7 0.2 copy-done.3
  27.9 0.2 broadcast_multiply_fusion.1
  28.2 3.5 %fusion.12 = f32[40,40]{0,1:T(8,128)S(1)} fusion(bf16[40,256,128]{2,1,0:T(8,128)(2,1)S(1)} %broadcast_multiply_fusion), kind=kOutput, calls=%fused_computation.13 | convolution fusion | flops 104857600 | bytes 2627840 | tf_op jit(solution)/shard_map/dot_general | solution.py:89
  31.7 0.2 pad.40
  32.0 2.7 %copy.53 = bf16[4,8,256,128]{3,1,2,0:T(8,128)(2,1)} copy(bf16[4,8,256,128]{3,2,1,0:T(8,128)(2,1)S(1)} %bitcast.115) | data formatting | bytes 4194304
  34.7 0.3 fusion.82
  35.0 0.5 collective-permute-start.2
  35.5 4.0 %collective-permute-start.3 = (f32[1,128]{1,0:T(1,128)S(1)}, f32[1,128]{1,0:T(1,128)S(1)}, u32[]{:S(2)}, u32[]{:S(2)}) collective-permute-start(f32[1,128]{1,0:T(1,128)S(1)} %get-tuple-element.24), channel_id=1, source_target_pairs={{1,0},{2,1},{3,2},{4,3},{5,4},{6,5},{7,6},{8,7},{9,8},{10,9},{11,1... | collective-permute-start | bytes 1544 | tf_op jit(solution)/shard_map/ppermute | solution.py:22
  39.5 0.1 fusion.89
  39.6 1.1 collective-permute-done.2
  40.7 0.1 collective-permute-done.3
  40.8 0.1 fusion.80
  41.0 4.4 %collective-permute-start.5 = (f32[1,128]{1,0:T(1,128)S(1)}, f32[1,128]{1,0:T(1,128)S(1)}, u32[]{:S(2)}, u32[]{:S(2)}) collective-permute-start(f32[1,128]{1,0:T(1,128)S(1)} %get-tuple-element.20), channel_id=1, source_target_pairs={{1,0},{2,1},{3,2},{4,3},{5,4},{6,5},{7,6},{8,7},{9,8},{10,9},{11,1... | collective-permute-start | bytes 1544 | tf_op jit(solution)/shard_map/ppermute | solution.py:22
  45.4 0.1 fusion.87
  45.5 1.1 collective-permute-done.4
  46.6 0.1 collective-permute-done.5
  46.7 0.1 fusion.78
  46.9 4.4 %collective-permute-start.7 = (f32[1,128]{1,0:T(1,128)S(1)}, f32[1,128]{1,0:T(1,128)S(1)}, u32[]{:S(2)}, u32[]{:S(2)}) collective-permute-start(f32[1,128]{1,0:T(1,128)S(1)} %get-tuple-element.16), channel_id=1, source_target_pairs={{1,0},{2,1},{3,2},{4,3},{5,4},{6,5},{7,6},{8,7},{9,8},{10,9},{11,1... | collective-permute-start | bytes 1544 | tf_op jit(solution)/shard_map/ppermute | solution.py:22
  51.3 0.1 fusion.85
  51.4 1.1 collective-permute-done.6
  52.6 0.7 fusion.76
  53.4 1.0 fusion.29
  54.4 5.8 %all-to-all-start.2 = ((f32[16,16,128]{2,1,0:T(8,128)}), f32[16,16,128]{2,1,0:T(8,128)S(1)}, u32[]{:S(2)}, u32[]{:S(2)}) async-start(f32[16,16,128]{2,1,0:T(8,128)} %bitcast.6), calls=%async_computation.2 | async-start | bytes 262144 | tf_op jit(solution)/shard_map/all_to_all | solution.py:82
  60.1 4.4 %fusion.15 = f32[30,30]{0,1:T(8,128)S(1)} fusion(bf16[30,256,128]{2,1,0:T(8,128)(2,1)} %copy-done.1), kind=kOutput, calls=%fused_computation.14 | convolution fusion | flops 58982400 | bytes 1969680 | tf_op jit(solution)/shard_map/dot_general | solution.py:93
  64.6 3.5 %all-to-all-done.2 = f32[16,16,128]{2,1,0:T(8,128)S(1)} async-done(((f32[16,16,128]{2,1,0:T(8,128)}), f32[16,16,128]{2,1,0:T(8,128)S(1)}, u32[]{:S(2)}, u32[]{:S(2)}) %all-to-all-start.2) | async-done | bytes 131104 | tf_op jit(solution)/shard_map/all_to_all | solution.py:82
  68.1 0.1 fusion.27
  68.2 2.1 %fusion.19 = f32[40]{0:T(128)S(1)} fusion(bf16[40,256,128]{2,1,0:T(8,128)(2,1)S(1)} %broadcast_multiply_fusion, bf16[256,128,1]{1,0,2:T(8,128)(2,1)S(1)} %bitcast.123), kind=kOutput, calls=%fused_computation.17 | convolution fusion | flops 2621440 | bytes 2687136 | tf_op jit(solution)/shard_map/dot_general | solution.py:92
  70.3 58.4 %all-reduce.9 = (f32[40,40]{0,1:T(8,128)S(1)}, f32[40]{0:T(128)S(1)}) all-reduce(f32[40,40]{0,1:T(8,128)S(1)} %fusion.12, f32[40]{0:T(128)S(1)} %fusion.19), channel_id=1, replica_groups=mesh['runs'=2,'tile'=16] {'tile'}, use_global_device_ids=true, to_apply=%region_2.0 | all-reduce | flops 1640 | bytes 13120 | tf_op jit(solution)/shard_map/psum | solution.py:96
  128.7 3.6 %cholesky.29 = f32[40,40]{1,0:T(8,128)S(1)} custom-call(f32[40,40]{1,0:T(8,128)S(1)} %fusion.64), custom_call_target="Cholesky" | custom-call | tf_op jit(solution)/shard_map/jit(cholesky)/cholesky | solution.py:37
  132.4 0.6 compare_reduce_fusion.1
  133.1 0.7 fusion.61
  133.7 3.1 %custom-call.16 = f32[1,40,40]{1,2,0:T(8,128)S(1)} custom-call(f32[1,40,40]{2,1,0:T(8,128)S(1)} %fusion.61), custom_call_target="InvertDiagBlocksLowerTriangular" | custom-call | tf_op jit(solution)/shard_map/triangular_solve | solution.py:39
  136.8 0.1 convolution_bitcast_fusion.3
  136.9 0.1 fusion.22
  137.1 2.4 %fusion = f32[1,32768]{1,0:T(1,128)S(1)} fusion(bf16[5,8,256,128]{3,2,1,0:T(8,128)(2,1)S(1)} %bitcast.113, f32[40]{0:T(128)S(1)} %fusion.22), kind=kOutput, calls=%fused_computation | convolution fusion | flops 15728640 | bytes 2752672 | tf_op jit(solution)/shard_map/dot_general | solution.py:98
  139.6 1.7 convolution_bitcast_fusion.4
  141.3 57.8 %all-reduce.8 = (f32[30,30]{0,1:T(8,128)S(1)}, f32[30]{0:T(128)S(1)}) all-reduce(f32[30,30]{0,1:T(8,128)S(1)} %fusion.15, f32[30]{0:T(128)S(1)} %convolution_bitcast_fusion.4), channel_id=1, replica_groups=mesh['runs'=2,'tile'=16] {'tile'}, use_global_device_ids=true, to_apply=%region_6.7 | all-reduce | flops 930 | bytes 7440 | tf_op jit(solution)/shard_map/psum | solution.py:96
  199.1 0.1 copy.46
  199.2 2.7 %cholesky.61 = f32[30,30]{1,0:T(8,128)S(1)} custom-call(f32[30,30]{1,0:T(8,128)S(1)} %fusion.68), custom_call_target="Cholesky" | custom-call | tf_op jit(solution)/shard_map/jit(cholesky)/cholesky | solution.py:37
  202.0 0.6 compare_reduce_fusion
  202.7 0.7 fusion.65
  203.3 2.3 %custom-call.17 = f32[1,30,30]{1,2,0:T(8,128)S(1)} custom-call(f32[1,30,30]{2,1,0:T(8,128)S(1)} %fusion.65), custom_call_target="InvertDiagBlocksLowerTriangular" | custom-call | tf_op jit(solution)/shard_map/triangular_solve | solution.py:39
  205.6 0.2 convolution_bitcast_fusion.1
  205.8 0.1 fusion.24
  205.9 3.5 %fusion.3 = f32[1,32768]{1,0:T(1,128)S(1)} fusion(bf16[5,8,256,128]{3,2,1,0:T(8,128)(2,1)} %bitcast.117, f32[40]{0:T(128)S(1)} %fusion.22), kind=kOutput, calls=%fused_computation.3 | convolution fusion | flops 2621480 | bytes 2752672 | tf_op jit(solution)/shard_map/dot_general | solution.py:105
  209.4 0.4 fusion.92
  209.8 0.8 fusion.25
  (33 shorter events, 0.4 us)
Async XLA Ops:
  1.3 33.3 %collective-permute-start = (f32[1,128]{1,0:T(1,128)S(1)}, f32[1,128]{1,0:T(1,128)S(1)}, u32[]{:S(2)}, u32[]{:S(2)}) collective-permute-start(f32[1,128]{1,0:T(1,128)S(1)} %get-tuple-element.27), channel_id=1, source_target_pairs={{0,1},{1,2},{2,3},{3,4},{4,5},{5,6},{6,7},{7,8},{8,9},{9,10},{10,1... | collective-permute-start | bytes 1544 | tf_op jit(solution)/shard_map/ppermute | solution.py:20
  1.8 32.9 %collective-permute-start.1 = (f32[1,128]{1,0:T(1,128)S(1)}, f32[1,128]{1,0:T(1,128)S(1)}, u32[]{:S(2)}, u32[]{:S(2)}) collective-permute-start(f32[1,128]{1,0:T(1,128)S(1)} %get-tuple-element.28), channel_id=1, source_target_pairs={{1,0},{2,1},{3,2},{4,3},{5,4},{6,5},{7,6},{8,7},{9,8},{10,9},{11,1... | collective-permute-start | bytes 1544 | tf_op jit(solution)/shard_map/ppermute | solution.py:22
  9.1 10.0 %all-to-all-start = ((f32[16,16,1]{1,2,0:T(1,128)}), f32[16,16,1]{1,2,0:T(1,128)S(1)}, u32[]{:S(2)}, u32[]{:S(2)}) async-start(f32[16,16,1]{1,2,0:T(1,128)} %bitcast.3), calls=%async_computation | async-start | bytes 16384 | tf_op jit(solution)/shard_map/all_to_all | solution.py:83
  19.2 15.5 %all-to-all-start.1 = ((f32[16,16,128]{2,1,0:T(8,128)}), f32[16,16,128]{2,1,0:T(8,128)S(1)}, u32[]{:S(2)}, u32[]{:S(2)}) async-start(f32[16,16,128]{2,1,0:T(8,128)} %bitcast.4), calls=%async_computation.1 | async-start | bytes 262144 | tf_op jit(solution)/shard_map/all_to_all | solution.py:71
  25.6 2.3 %copy-start.3 = (bf16[30,256,128]{2,1,0:T(8,128)(2,1)S(1)}, bf16[30,256,128]{2,1,0:T(8,128)(2,1)}, u32[]{:S(2)}) copy-start(bf16[30,256,128]{2,1,0:T(8,128)(2,1)} %param.18) | copy-start | bytes 5898244
  28.1 3.8 %copy-start.1 = (bf16[30,256,128]{2,1,0:T(8,128)(2,1)}, bf16[30,256,128]{2,1,0:T(8,128)(2,1)S(1)}, u32[]{:S(2)}) copy-start(bf16[30,256,128]{2,1,0:T(8,128)(2,1)S(1)} %broadcast_multiply_fusion.1) | copy-start | bytes 5898244
  32.0 2.7 %copy-start.4 = (f32[128,128]{1,0:T(8,128)S(1)}, f32[128,128]{1,0:T(8,128)}, u32[]{:S(2)}) copy-start(f32[128,128]{1,0:T(8,128)} %param.14) | copy-start | bytes 196612
  32.0 2.7 %copy-start.5 = (f32[128,128]{1,0:T(8,128)S(1)}, f32[128,128]{1,0:T(8,128)}, u32[]{:S(2)}) copy-start(f32[128,128]{1,0:T(8,128)} %param.12) | copy-start | bytes 196612
  32.0 2.7 %copy-start.8 = (f32[128,128]{1,0:T(8,128)S(1)}, f32[128,128]{1,0:T(8,128)}, u32[]{:S(2)}) copy-start(f32[128,128]{1,0:T(8,128)} %param.13) | copy-start | bytes 196612
  35.0 5.7 %collective-permute-start.2 = (f32[1,128]{1,0:T(1,128)S(1)}, f32[1,128]{1,0:T(1,128)S(1)}, u32[]{:S(2)}, u32[]{:S(2)}) collective-permute-start(f32[1,128]{1,0:T(1,128)S(1)} %get-tuple-element.23), channel_id=1, source_target_pairs={{0,1},{1,2},{2,3},{3,4},{4,5},{5,6},{6,7},{7,8},{8,9},{9,10},{10,1... | collective-permute-start | bytes 1544 | tf_op jit(solution)/shard_map/ppermute | solution.py:20
  35.5 5.3 %collective-permute-start.3 = (f32[1,128]{1,0:T(1,128)S(1)}, f32[1,128]{1,0:T(1,128)S(1)}, u32[]{:S(2)}, u32[]{:S(2)}) collective-permute-start(f32[1,128]{1,0:T(1,128)S(1)} %get-tuple-element.24), channel_id=1, source_target_pairs={{1,0},{2,1},{3,2},{4,3},{5,4},{6,5},{7,6},{8,7},{9,8},{10,9},{11,1... | collective-permute-start | bytes 1544 | tf_op jit(solution)/shard_map/ppermute | solution.py:22
  40.9 5.7 %collective-permute-start.4 = (f32[1,128]{1,0:T(1,128)S(1)}, f32[1,128]{1,0:T(1,128)S(1)}, u32[]{:S(2)}, u32[]{:S(2)}) collective-permute-start(f32[1,128]{1,0:T(1,128)S(1)} %get-tuple-element.19), channel_id=1, source_target_pairs={{0,1},{1,2},{2,3},{3,4},{4,5},{5,6},{6,7},{7,8},{8,9},{9,10},{10,1... | collective-permute-start | bytes 1544 | tf_op jit(solution)/shard_map/ppermute | solution.py:20
  41.0 5.7 %collective-permute-start.5 = (f32[1,128]{1,0:T(1,128)S(1)}, f32[1,128]{1,0:T(1,128)S(1)}, u32[]{:S(2)}, u32[]{:S(2)}) collective-permute-start(f32[1,128]{1,0:T(1,128)S(1)} %get-tuple-element.20), channel_id=1, source_target_pairs={{1,0},{2,1},{3,2},{4,3},{5,4},{6,5},{7,6},{8,7},{9,8},{10,9},{11,1... | collective-permute-start | bytes 1544 | tf_op jit(solution)/shard_map/ppermute | solution.py:22
  46.7 21.3 %copy-start.7 = (f32[256,128]{1,0:T(8,128)S(1)}, f32[256,128]{1,0:T(8,128)}, u32[]{:S(2)}) copy-start(f32[256,128]{1,0:T(8,128)} %param.11) | copy-start | bytes 393220
  46.8 5.7 %collective-permute-start.6 = (f32[1,128]{1,0:T(1,128)S(1)}, f32[1,128]{1,0:T(1,128)S(1)}, u32[]{:S(2)}, u32[]{:S(2)}) collective-permute-start(f32[1,128]{1,0:T(1,128)S(1)} %get-tuple-element.15), channel_id=1, source_target_pairs={{0,1},{1,2},{2,3},{3,4},{4,5},{5,6},{6,7},{7,8},{8,9},{9,10},{10,1... | collective-permute-start | bytes 1544 | tf_op jit(solution)/shard_map/ppermute | solution.py:20
  46.9 5.7 %collective-permute-start.7 = (f32[1,128]{1,0:T(1,128)S(1)}, f32[1,128]{1,0:T(1,128)S(1)}, u32[]{:S(2)}, u32[]{:S(2)}) collective-permute-start(f32[1,128]{1,0:T(1,128)S(1)} %get-tuple-element.16), channel_id=1, source_target_pairs={{1,0},{2,1},{3,2},{4,3},{5,4},{6,5},{7,6},{8,7},{9,8},{10,9},{11,1... | collective-permute-start | bytes 1544 | tf_op jit(solution)/shard_map/ppermute | solution.py:22
  53.3 16.9 %copy-start.6 = (f32[128,128]{1,0:T(8,128)}, f32[128,128]{1,0:T(8,128)S(1)}, u32[]{:S(2)}) copy-start(f32[128,128]{1,0:T(8,128)S(1)} %get-tuple-element.7) | copy-start | bytes 196612
  54.4 13.7 %all-to-all-start.2 = ((f32[16,16,128]{2,1,0:T(8,128)}), f32[16,16,128]{2,1,0:T(8,128)S(1)}, u32[]{:S(2)}, u32[]{:S(2)}) async-start(f32[16,16,128]{2,1,0:T(8,128)} %bitcast.6), calls=%async_computation.2 | async-start | bytes 262144 | tf_op jit(solution)/shard_map/all_to_all | solution.py:82
  136.8 2.8 %copy-start.2 = (bf16[4,8,256,128]{3,1,2,0:T(8,128)(2,1)S(1)}, bf16[4,8,256,128]{3,1,2,0:T(8,128)(2,1)}, u32[]{:S(2)}) copy-start(bf16[4,8,256,128]{3,1,2,0:T(8,128)(2,1)} %copy.53) | copy-start | bytes 6291460
  139.6 69.8 %copy-start = (bf16[4,8,256,128]{3,1,2,0:T(8,128)(2,1)S(1)}, bf16[4,8,256,128]{3,1,2,0:T(8,128)(2,1)}, u32[]{:S(2)}) copy-start(bf16[4,8,256,128]{3,1,2,0:T(8,128)(2,1)} %copy.55) | copy-start | bytes 6291460
where the time goes:
time: 211 us
  blocking collectives  116 us (55%)
  starting transfers between devices  33.5 us (16%)
  matrix products  20.9 us (10%)
  other arithmetic  20 us (9%)
  local copies, waits for them, and re-layouts  11 us (5%)
  waiting for transfers between devices  8.01 us (4%)
    psum x2, blocking collectives, local(): lax.psum((gram_cur, rhs_cur, gram_past), 'tile')  116 us
    ppermute x4, starting transfers between devices, padded_2(): lax.ppermute(head, axis, [((i + 1) % count, i) for i in range(count)])  17.9 us
    another operation x6, other arithmetic, solve_spd(): factor = jnp.linalg.cholesky(matrix)  7.73 us
    unnamed x22, local copies, waits for them, and re-layouts  7.61 us
    another operation x4, other arithmetic, solve_spd(): lax.linalg.triangular_solve(factor, inner, left_side=True, lower=True, tr...  6.64 us
    all_to_all x1, starting transfers between devices, local(): lax.all_to_all(outgoing, 'tile', split_axis=0, concat_axis=0, tiled=True)  5.76 us
    all_to_all x1, starting transfers between devices, local(): lax.all_to_all(fluid_press, 'tile', split_axis=0, concat_axis=0, tiled=True)  5.15 us
    dot_general x1, matrix products, local(): lax.dot_general(past_cols, past_cols, (((1,), (1,)), ((), ())), preferred...  4.43 us
  transfers between devices with their start and end apart: 11, of which 8 were waited for; matrix products, arithmetic and copies ran while one was open for 10% of the time, Pallas kernels for 0%

commit v1 on v0

v1 whole, which is shorter than its diff:
```python
import functools

import jax
import jax.numpy as jnp
from jax import lax
from jax.experimental import pallas as pl
from jax.experimental.pallas import tpu as pltpu
from jax.sharding import PartitionSpec as P

SUBSTEPS = 4
DAMPING = 0.05
EDGE = 8
F32 = jnp.float32
BF16 = jnp.bfloat16


def split3(x):
    hi = x.astype(BF16)
    rest = x - hi.astype(F32)
    mid = rest.astype(BF16)
    low = (rest - mid.astype(F32)).astype(BF16)
    return hi, mid, low


def dot(a, b, dims=((1,), (0,))):
    return lax.dot_general(a, b, (dims, ((), ())), preferred_element_type=F32)


def iota(shape, axis):
    return lax.broadcasted_iota(jnp.int32, shape, axis)


def kernel(
    n, per, wide,
    press, iterate, displace, velocity, stiffness, owners, diff_cur, step_cur, diff_past, step_past,
    new_ref, field_ref, speed_ref,
    vd, vs, ext, pext, cnt, stage, pbuf, obuf, xbuf, gram, rsbuf, agbuf, prow, arbuf, elim, coefs,
    load_sem, send_sem, recv_sem, halo_send, halo_recv,
):
    me = lax.axis_index("tile")
    left, right = lax.rem(me + n - 1, n), lax.rem(me + 1, n)
    lines = displace.shape[0]
    slots = iterate.shape[0]
    nc, npast = diff_cur.shape[0], diff_past.shape[0]
    cols = vd.shape[0]
    total = n * wide

    def peers(fn):
        def step(i, carry):
            fn(lax.rem(me + i, n))
            return carry

        lax.fori_loop(1, n, step, 0)

    barrier = pltpu.get_barrier_semaphore()
    peers(lambda p: pl.semaphore_signal(
        barrier, inc=1, device_id={"tile": p}, device_id_type=pl.DeviceIdType.MESH))

    loads = [
        pltpu.make_async_copy(diff_cur, vd.at[pl.ds(0, nc)], load_sem.at[0]),
        pltpu.make_async_copy(diff_past, vd.at[pl.ds(nc, npast)], load_sem.at[1]),
        pltpu.make_async_copy(step_cur, vs.at[pl.ds(0, nc)], load_sem.at[2]),
        pltpu.make_async_copy(step_past, vs.at[pl.ds(nc, npast)], load_sem.at[3]),
    ]
    for load in loads:
        load.start()

    def send(src, dst, phase, p):
        pltpu.make_async_remote_copy(
            src_ref=src, dst_ref=dst, send_sem=send_sem.at[phase], recv_sem=recv_sem.at[phase],
            device_id={"tile": p}, device_id_type=pl.DeviceIdType.MESH).start()

    def wait(buf, sem):
        part = buf.at[pl.ds(0, n - 1)]
        pltpu.make_async_copy(part, part, sem).wait()

    ext[0, EDGE:EDGE + lines, :] = displace[...]
    ext[1, EDGE:EDGE + lines, :] = velocity[...]
    ext[2, EDGE:EDGE + lines, :] = stiffness[...]
    own = owners[...].astype(F32)
    lane_f = iota((lines, 128), 1).astype(F32)
    onehot = jnp.where(own == lane_f, 1.0, 0.0)
    cnt[me] = jnp.broadcast_to(jnp.sum(onehot, axis=0, keepdims=True), (8, 128))
    if wide != per:
        stage[...] = jnp.zeros_like(stage)
        for s in range(n):
            stage[s, 0:per, :] = press[s * per:(s + 1) * per, :]

    pl.semaphore_wait(barrier, n - 1)
    peers(lambda p: send(cnt.at[me], cnt.at[me], 0, p))

    def press_block(p):
        if wide != per:
            return stage.at[p]
        return press.at[pl.ds(pl.multiple_of(p * per, 8), per)]

    peers(lambda p: send(press_block(p), pbuf.at[me], 1, p))
    if wide != per:
        pbuf[me] = stage[me]
    else:
        pbuf[me] = press[pl.ds(pl.multiple_of(me * per, 8), per), :]

    def halos(buf, first, lead):
        moves = []
        for k, (src, dst, who) in enumerate((
            (EDGE, EDGE + lines, left),
            (lines, 0, right),
        )):
            moves.append(pltpu.make_async_remote_copy(
                src_ref=buf.at[lead + (pl.ds(src, EDGE),)], dst_ref=buf.at[lead + (pl.ds(dst, EDGE),)],
                send_sem=halo_send.at[first + k], recv_sem=halo_recv.at[first + k],
                device_id={"tile": who}, device_id_type=pl.DeviceIdType.MESH))
        for move in moves:
            move.start()
        return moves

    field_halo = halos(ext, 0, (slice(None),))

    below = jnp.where(iota((lines, lines), 0) > iota((lines, lines), 1), 1.0, 0.0).astype(BF16)
    earlier = dot(below, onehot.astype(BF16))
    rank = jnp.sum(earlier * onehot, axis=1, keepdims=True)
    slot = own * float(wide) + rank
    chooser = jnp.where(slot == iota((lines, total), 1).astype(F32), 1.0, 0.0).astype(BF16)
    same = iota((lines, lines), 0) == iota((lines, lines), 1)
    slot_row = jnp.sum(jnp.where(same, slot, 0.0), axis=0, keepdims=True)
    placer = jnp.where(slot_row == iota((total, lines), 0).astype(F32), 1.0, 0.0).astype(BF16)

    vd[nc + npast:cols] = jnp.zeros((cols - nc - npast, slots, 128), BF16)
    gram[...] = jnp.zeros_like(gram)
    prow[...] = jnp.zeros_like(prow)

    wait(cnt, recv_sem.at[0])
    mine = jnp.sum(jnp.where(iota((n, 8, 128), 2) == me, cnt[...], 0.0), axis=2, keepdims=True)
    mine = jnp.broadcast_to(mine, (n, 8, 128))
    if wide > 8:
        mine = jnp.concatenate([mine] * (wide // 8), axis=1)
    mask3 = jnp.where(iota((n, wide, 128), 1).astype(F32) < mine, 1.0, 0.0)

    def compact(cells):
        if wide == per:
            return cells.reshape(slots, 128)
        return jnp.concatenate([cells[s, 0:per, :] for s in range(n)], axis=0)

    mask = compact(mask3)
    mask_half = mask.astype(BF16)

    loads[0].wait()
    loads[1].wait()

    def apply_mask(k, carry):
        vd[k] = vd[k] * mask_half
        return carry

    lax.fori_loop(0, nc + npast, apply_mask, 0)

    def gather(a):
        return jnp.concatenate([
            vd[pl.ds(a * 16, 16), r * 16:(r + 1) * 16, :].reshape(256, 128)
            for r in range(slots // 16)], axis=1)

    def outer(a, carry):
        def inner(b, carry):
            prod = dot(gather(a), gather(b), ((1,), (1,)))
            alike = (iota((256, 256), 0) & 15) == (iota((256, 256), 1) & 15)
            kept = jnp.where(alike, prod, 0.0).reshape(16, 16, 256)
            kept = jnp.sum(kept, axis=1) * jnp.where(a == b, 0.5, 1.0)
            spread = jnp.where((iota((256, 128), 0) >> 4) + b * 16 == iota((256, 128), 1), 1.0, 0.0)
            spread = spread.astype(BF16)
            hi, mid, low = split3(kept)
            value = dot(hi, spread) + dot(mid, spread) + dot(low, spread)
            gram[pl.ds(2 * a, 2)] += value.reshape(2, 8, 128)
            return carry

        return lax.fori_loop(a, cols // 16, inner, carry)

    lax.fori_loop(0, cols // 16, outer, 0)
    peers(lambda p: send(gram.at[p], rsbuf.at[me], 2, p))
    rsbuf[me] = gram[me]

    wait(pbuf, recv_sem.at[1])
    returned = pbuf[...].reshape(total, 128)
    hi, mid, low = split3(returned)
    pext[EDGE:EDGE + lines, :] = dot(chooser, hi) + dot(chooser, mid) + dot(chooser, low)
    press_halo = halos(pext, 2, ())

    wait(rsbuf, recv_sem.at[2])
    agbuf[me] = jnp.sum(rsbuf[...], axis=0)
    peers(lambda p: send(agbuf.at[me], agbuf.at[me], 3, p))

    for move in field_halo:
        move.wait()
    for move in press_halo:
        move.wait()
    w, v, stiff, force = ext[0], ext[1], ext[2], pext[...]
    rows = lines + 2 * EDGE
    lane = iota((rows, 128), 1)
    for _ in range(SUBSTEPS):
        upper = pltpu.roll(w, 1, 0)
        beneath = pltpu.roll(w, rows - 1, 0)
        lft = jnp.where(lane == 0, 0.0, pltpu.roll(w, 1, 1))
        rgt = jnp.where(lane == 127, 0.0, pltpu.roll(w, 127, 1))
        lapl = upper + beneath + (lft + rgt) - 4.0 * w
        v = v + (stiff * lapl + force - DAMPING * v)
        w = w + v
    field = w[EDGE:EDGE + lines, :]
    hi, mid, low = split3(field)
    placed = dot(placer, hi) + dot(placer, mid) + dot(placer, low)
    obuf[...] = placed.reshape(n, wide, 128)
    peers(lambda p: send(obuf.at[p], xbuf.at[me], 4, p))
    xbuf[me] = obuf[me]
    field_ref[...] = field
    speed_ref[...] = v[EDGE:EDGE + lines, :]

    wait(agbuf, recv_sem.at[3])
    half = agbuf[0:16].reshape(128, 128)
    full = half + half.T
    lane2, sub2 = iota((nc, 128), 1), iota((nc, 128), 0)
    unit = jnp.where(lane2 == sub2 + 64, 1.0, 0.0)
    cross = full[nc:2 * nc, :]
    past_part = jnp.where(lane2 < nc, pltpu.roll(cross, 128 - nc, 1), 0.0)
    elim[0] = jnp.where(lane2 < nc, full[0:nc, :], 0.0) + unit
    elim[1] = past_part + unit + jnp.where((lane2 == sub2) & (sub2 >= npast), 1.0, 0.0)
    lane3, sub3 = iota((2, nc, 128), 2), iota((2, nc, 128), 1)

    def eliminate(j, carry):
        now = elim[...]
        row = elim[:, pl.ds(j, 1), :]
        col = jnp.sum(jnp.where(lane3 == j, now, 0.0), axis=2, keepdims=True)
        pivot = jnp.sum(jnp.where(iota((2, 1, 128), 2) == j, row, 0.0), axis=2, keepdims=True)
        elim[...] = jnp.where(sub3 > j, now - col * (row / pivot), now)
        return carry

    lax.fori_loop(0, nc, eliminate, 0)
    done = elim[...]
    diag2 = lane2 == sub2
    inverse, pivots = [], []
    for part in range(2):
        inverse.append(jnp.where(lane2 < nc, pltpu.roll(done[part], 64, 1), 0.0))
        pivots.append(jnp.sum(jnp.where(diag2, done[part], 0.0), axis=1, keepdims=True))

    wait(xbuf, recv_sem.at[4])
    x_tilde = compact(xbuf[...])
    resid = (mask * (x_tilde - iterate[...])).astype(BF16).astype(F32)

    def product(k, carry):
        prow[pl.ds(k, 1), :] = jnp.sum(vd[k].astype(F32) * resid, axis=0, keepdims=True)
        return carry

    lax.fori_loop(0, nc + npast, product, 0)
    ones = jnp.ones((8, 128), BF16)
    hi, mid, low = split3(prow[...])
    arbuf[me] = (dot(ones, hi, ((1,), (1,))) + dot(ones, mid, ((1,), (1,)))
                 + dot(ones, low, ((1,), (1,))))
    peers(lambda p: send(arbuf.at[me], arbuf.at[me], 5, p))
    loads[2].wait()
    loads[3].wait()
    wait(arbuf, recv_sem.at[5])
    rhs = jnp.sum(arbuf[...], axis=0)

    def solve(part, vector):
        inner = jnp.sum(inverse[part] * vector, axis=1, keepdims=True) / pivots[part]
        return jnp.sum(inverse[part] * inner, axis=0, keepdims=True)

    coeff = -solve(0, rhs[0:1, :])
    carried = jnp.sum(cross * coeff, axis=1, keepdims=True)
    carried = jnp.sum(jnp.where(diag2, carried, 0.0), axis=0, keepdims=True)
    past = solve(1, pltpu.roll(rhs, 128 - nc, 1)[0:1, :] + carried)
    for part, vector in enumerate((coeff, -past)):
        column = jnp.sum(jnp.where(diag2, vector, 0.0), axis=1, keepdims=True)
        coefs[part * nc:(part + 1) * nc, :] = jnp.broadcast_to(
            column, (nc, 128)).astype(BF16).astype(F32)

    def accumulate(k, acc):
        return acc + coefs[pl.ds(k, 1), :] * vs[k].astype(F32)

    update = lax.fori_loop(0, nc + npast, accumulate, jnp.zeros((slots, 128), F32))
    new_ref[...] = mask * (x_tilde + update)

    for phase, buf in enumerate((cnt, pbuf, rsbuf, agbuf, xbuf, arbuf)):
        wait(buf, send_sem.at[phase])


def local(press, iterate, displace, velocity, stiffness, owners, diff_cur, step_cur, diff_past, step_past):
    n = lax.axis_size("tile")
    lines, slots = displace.shape[0], iterate.shape[0]
    per = slots // n
    wide = max(8, per)
    nc, npast = diff_cur.shape[0], diff_past.shape[0]
    cols = -(-2 * nc // 16) * 16
    vmem = pl.BlockSpec(memory_space=pltpu.VMEM)
    hbm = pl.BlockSpec(memory_space=pl.ANY)
    tiles = pltpu.VMEM((n, 8, 128), F32)
    blocks = pltpu.VMEM((n, wide, 128), F32)
    return pl.pallas_call(
        functools.partial(kernel, n, per, wide),
        out_shape=(
            jax.ShapeDtypeStruct((slots, 128), F32),
            jax.ShapeDtypeStruct((lines, 128), F32),
            jax.ShapeDtypeStruct((lines, 128), F32),
        ),
        in_specs=[vmem] * 6 + [hbm] * 4,
        out_specs=(vmem, vmem, vmem),
        scratch_shapes=[
            pltpu.VMEM((cols, slots, 128), BF16),
            pltpu.VMEM((nc + npast, slots, 128), BF16),
            pltpu.VMEM((3, lines + 2 * EDGE, 128), F32),
            pltpu.VMEM((lines + 2 * EDGE, 128), F32),
            tiles,
            blocks if wide != per else pltpu.VMEM((8, 128), F32),
            blocks, blocks, blocks,
            tiles, tiles, tiles,
            pltpu.VMEM((128, 128), F32),
            tiles,
            pltpu.VMEM((2, nc, 128), F32),
            pltpu.VMEM((2 * nc, 128), F32),
            pltpu.SemaphoreType.DMA((4,)),
            pltpu.SemaphoreType.DMA((6,)),
            pltpu.SemaphoreType.DMA((6,)),
            pltpu.SemaphoreType.DMA((4,)),
            pltpu.SemaphoreType.DMA((4,)),
        ],
        compiler_params=pltpu.CompilerParams(
            collective_id=0, has_side_effects=True, vmem_limit_bytes=44 * 1024 * 1024),
    )(press, iterate, displace, velocity, stiffness, owners, diff_cur, step_cur, diff_past, step_past)


def solution(mesh):
    rows = P(("runs", "tile"), None)
    deep = P(None, ("runs", "tile"), None)
    return jax.shard_map(
        local,
        mesh=mesh,
        in_specs=(rows,) * 6 + (deep,) * 4,
        out_specs=(rows, rows, rows),
        check_vma=False,
    )
```

time: 211 us -> 59.5 us (0.28)
  blocking collectives: 116 us -> 0 us
  Pallas kernels: 0 us -> 44.9 us
  starting transfers between devices: 33.5 us -> 0 us
  matrix products: 20.9 us -> 0 us
  other arithmetic: 20 us -> 0 us
  waiting for transfers between devices: 8.01 us -> 0 us
  local copies, waits for them, and re-layouts: 11 us -> 13.6 us
    psum x2 -> x0, blocking collectives: 116 us -> none  [local(): lax.psum((gram_cur, rhs_cur, gram_past), 'tile')]
    pallas_call x0 -> x1, Pallas kernels: none -> 44.9 us  [local(): pl.pallas_call(functools.partial(kernel, n, per, wide), out_shape=(jax.Sh...]
    dot_general x10 -> x0, matrix products: 20.3 us -> none  [the longest x1 4.43 us: local(): lax.dot_general(past_cols, past_cols, (((1,), (1,)), ((), ())), preferred...]
    ppermute x8 -> x0, starting transfers between devices: 18.9 us -> none  [the longest x4 17.9 us: padded_2(): lax.ppermute(head, axis, [((i + 1) % count, i) for i in range(count)])]
    all_to_all x3 -> x0, starting transfers between devices: 14.6 us -> none  [the longest x1 5.76 us: local(): lax.all_to_all(outgoing, 'tile', split_axis=0, concat_axis=0, tiled=True)]
    another operation x10 -> x0, other arithmetic: 14.4 us -> none  [the longest x6 7.73 us: solve_spd(): factor = jnp.linalg.cholesky(matrix)]
    unnamed x22, local copies, waits for them, and re-layouts: 7.61 us -> 13.6 us
    all_to_all x3 -> x0, waiting for transfers between devices: 4.36 us -> none  [the longest x1 3.5 us: local(): lax.all_to_all(outgoing, 'tile', split_axis=0, concat_axis=0, tiled=True)]
  transfers between devices with their start and end apart: 11 -> 0, of which waited for: 8 -> 0; matrix products, arithmetic and copies ran while one was open for 10% -> 0% of each run, Pallas kernels for 0% -> 0%
where the time goes in v1:
time: 59.5 us; the launch traced here: 59.1 us
  Pallas kernels  44.9 us (75%)
  local copies, waits for them, and re-layouts  13.6 us (23%)
  between operations  0.65 us (1%)
    pallas_call x1, Pallas kernels, local(): pl.pallas_call(functools.partial(kernel, n, per, wide), out_shape=(jax.Sh...  44.9 us
    unnamed x22, local copies, waits for them, and re-layouts  13.6 us

profile of v1, /device:TPU:0, one launch (start us, length us, event | category | flops | bytes accessed | tf_op | source)
XLA Modules:
  0.0 59.1 jit_solution(9387010486819507546)
XLA Ops:
  0.6 0.8 %copy.13.owners = s32[128,1]{1,0:T(8,128)S(1)} copy(s32[128,1]{0,1:T(1,128)} %param.15) | data formatting | bytes 1024 | tf_op args[5]
  1.4 0.0 copy-start
  1.4 1.7 %copy-done = bf16[40,256,128]{2,1,0:T(8,128)(2,1)S(1)} copy-done((bf16[40,256,128]{2,1,0:T(8,128)(2,1)S(1)}, bf16[40,256,128]{2,1,0:T(8,128)(2,1)}, u32[]{:S(2)}) %copy-start) | copy-done | bytes 2621464
  3.1 0.0 copy-start.1
  3.1 1.7 %copy-done.1 = bf16[40,256,128]{2,1,0:T(8,128)(2,1)S(1)} copy-done((bf16[40,256,128]{2,1,0:T(8,128)(2,1)S(1)}, bf16[40,256,128]{2,1,0:T(8,128)(2,1)}, u32[]{:S(2)}) %copy-start.1) | copy-done | bytes 2621464
  4.9 0.0 copy-start.2
  4.9 1.5 %copy-done.2 = bf16[30,256,128]{2,1,0:T(8,128)(2,1)S(1)} copy-done((bf16[30,256,128]{2,1,0:T(8,128)(2,1)S(1)}, bf16[30,256,128]{2,1,0:T(8,128)(2,1)}, u32[]{:S(2)}) %copy-start.2) | copy-done | bytes 1966104
  6.4 0.0 copy-start.3
  6.4 1.5 %copy-done.3 = bf16[30,256,128]{2,1,0:T(8,128)(2,1)S(1)} copy-done((bf16[30,256,128]{2,1,0:T(8,128)(2,1)S(1)}, bf16[30,256,128]{2,1,0:T(8,128)(2,1)}, u32[]{:S(2)}) %copy-start.3) | copy-done | bytes 1966104
  8.0 0.0 copy-start.4
  8.0 0.9 %copy-done.4 = f32[256,128]{1,0:T(8,128)S(1)} copy-done((f32[256,128]{1,0:T(8,128)S(1)}, f32[256,128]{1,0:T(8,128)}, u32[]{:S(2)}) %copy-start.4) | copy-done | bytes 131096
  8.9 0.0 copy-start.5
  8.9 0.9 %copy-done.5 = f32[256,128]{1,0:T(8,128)S(1)} copy-done((f32[256,128]{1,0:T(8,128)S(1)}, f32[256,128]{1,0:T(8,128)}, u32[]{:S(2)}) %copy-start.5) | copy-done | bytes 131096
  9.8 0.0 copy-start.6
  9.8 0.8 %copy-done.6 = f32[128,128]{1,0:T(8,128)S(1)} copy-done((f32[128,128]{1,0:T(8,128)S(1)}, f32[128,128]{1,0:T(8,128)}, u32[]{:S(2)}) %copy-start.6) | copy-done | bytes 65560
  10.6 0.0 copy-start.7
  10.6 0.8 %copy-done.7 = f32[128,128]{1,0:T(8,128)S(1)} copy-done((f32[128,128]{1,0:T(8,128)S(1)}, f32[128,128]{1,0:T(8,128)}, u32[]{:S(2)}) %copy-start.7) | copy-done | bytes 65560
  11.5 0.0 copy-start.8
  11.5 0.8 %copy-done.8 = f32[128,128]{1,0:T(8,128)S(1)} copy-done((f32[128,128]{1,0:T(8,128)S(1)}, f32[128,128]{1,0:T(8,128)}, u32[]{:S(2)}) %copy-start.8) | copy-done | bytes 65560
  12.3 44.9 %shard_map.121 = (f32[256,128]{1,0:T(8,128)S(1)}, f32[128,128]{1,0:T(8,128)S(1)}, f32[128,128]{1,0:T(8,128)S(1)}) custom-call(f32[256,128]{1,0:T(8,128)S(1)} %copy-done.4, f32[256,128]{1,0:T(8,128)S(1)} %copy-done.5, f32[128,128]{1,0:T(8,128)S(1)} %copy-done.6, f32[128,128]{1,0:T(8,128)S(1)} %copy-done.7, f32[128,128]{1,0:T(8,128)S(1)} %copy-done.8, ...), custom_call_target="tpu_custom_call" | custom-call | tf_op jit(solution)/shard_map/pallas_call | solution.py:294
  57.2 0.7 %copy.17 = f32[256,128]{1,0:T(8,128)} copy(f32[256,128]{1,0:T(8,128)S(1)} %get-tuple-element.6) | data formatting | bytes 262144
  57.8 0.6 %copy.18 = f32[128,128]{1,0:T(8,128)} copy(f32[128,128]{1,0:T(8,128)S(1)} %get-tuple-element.7) | data formatting | bytes 131072
  58.5 0.6 %copy.19 = f32[128,128]{1,0:T(8,128)} copy(f32[128,128]{1,0:T(8,128)S(1)} %get-tuple-element.8) | data formatting | bytes 131072
Async XLA Ops:
  1.4 1.7 %copy-start = (bf16[40,256,128]{2,1,0:T(8,128)(2,1)S(1)}, bf16[40,256,128]{2,1,0:T(8,128)(2,1)}, u32[]{:S(2)}) copy-start(bf16[40,256,128]{2,1,0:T(8,128)(2,1)} %diff_cur.1) | copy-start | bytes 7864324
  3.1 1.7 %copy-start.1 = (bf16[40,256,128]{2,1,0:T(8,128)(2,1)S(1)}, bf16[40,256,128]{2,1,0:T(8,128)(2,1)}, u32[]{:S(2)}) copy-start(bf16[40,256,128]{2,1,0:T(8,128)(2,1)} %step_cur.1) | copy-start | bytes 7864324
  4.9 1.5 %copy-start.2 = (bf16[30,256,128]{2,1,0:T(8,128)(2,1)S(1)}, bf16[30,256,128]{2,1,0:T(8,128)(2,1)}, u32[]{:S(2)}) copy-start(bf16[30,256,128]{2,1,0:T(8,128)(2,1)} %diff_past.1) | copy-start | bytes 5898244
  6.4 1.5 %copy-start.3 = (bf16[30,256,128]{2,1,0:T(8,128)(2,1)S(1)}, bf16[30,256,128]{2,1,0:T(8,128)(2,1)}, u32[]{:S(2)}) copy-start(bf16[30,256,128]{2,1,0:T(8,128)(2,1)} %step_past.1) | copy-start | bytes 5898244
  8.0 0.9 %copy-start.4 = (f32[256,128]{1,0:T(8,128)S(1)}, f32[256,128]{1,0:T(8,128)}, u32[]{:S(2)}) copy-start(f32[256,128]{1,0:T(8,128)} %press.1) | copy-start | bytes 393220
  8.9 0.9 %copy-start.5 = (f32[256,128]{1,0:T(8,128)S(1)}, f32[256,128]{1,0:T(8,128)}, u32[]{:S(2)}) copy-start(f32[256,128]{1,0:T(8,128)} %iterate.1) | copy-start | bytes 393220
  9.8 0.8 %copy-start.6 = (f32[128,128]{1,0:T(8,128)S(1)}, f32[128,128]{1,0:T(8,128)}, u32[]{:S(2)}) copy-start(f32[128,128]{1,0:T(8,128)} %displace.1) | copy-start | bytes 196612
  10.6 0.8 %copy-start.7 = (f32[128,128]{1,0:T(8,128)S(1)}, f32[128,128]{1,0:T(8,128)}, u32[]{:S(2)}) copy-start(f32[128,128]{1,0:T(8,128)} %velocity.1) | copy-start | bytes 196612
  11.5 0.8 %copy-start.8 = (f32[128,128]{1,0:T(8,128)S(1)}, f32[128,128]{1,0:T(8,128)}, u32[]{:S(2)}) copy-start(f32[128,128]{1,0:T(8,128)} %stiffness.1) | copy-start | bytes 196612

commit v2 on v1

--- a/solution.py
+++ b/solution.py
@@ -34,8 +34,8 @@
     n, per, wide,
     press, iterate, displace, velocity, stiffness, owners, diff_cur, step_cur, diff_past, step_past,
     new_ref, field_ref, speed_ref,
-    vd, vs, ext, pext, cnt, stage, pbuf, obuf, xbuf, gram, rsbuf, agbuf, prow, arbuf, elim, coefs,
-    load_sem, send_sem, recv_sem, halo_send, halo_recv,
+    vd, vs, masked, halfmask, iter_v, own_v, ext, pext, cnt, raw, stage, pbuf, obuf, xbuf, gram, rsbuf, agbuf, prow, arbuf, elim, coefs,
+    load_sem, small_sem, send_sem, recv_sem, halo_send, halo_recv,
 ):
     me = lax.axis_index("tile")
     left, right = lax.rem(me + n - 1, n), lax.rem(me + 1, n)
@@ -62,7 +62,19 @@
         pltpu.make_async_copy(step_cur, vs.at[pl.ds(0, nc)], load_sem.at[2]),
         pltpu.make_async_copy(step_past, vs.at[pl.ds(nc, npast)], load_sem.at[3]),
     ]
-    for load in loads:
+    small = [
+        pltpu.make_async_copy(owners, own_v, small_sem.at[0]),
+        pltpu.make_async_copy(displace, ext.at[0, pl.ds(EDGE, lines)], small_sem.at[1]),
+        pltpu.make_async_copy(velocity, ext.at[1, pl.ds(EDGE, lines)], small_sem.at[2]),
+        pltpu.make_async_copy(stiffness, ext.at[2, pl.ds(EDGE, lines)], small_sem.at[3]),
+        pltpu.make_async_copy(iterate, iter_v, small_sem.at[4]),
+    ]
+    if wide != per:
+        small.append(pltpu.make_async_copy(press, raw, small_sem.at[5]))
+    else:
+        small.append(pltpu.make_async_copy(
+            press.at[pl.ds(pl.multiple_of(me * per, 8), per)], pbuf.at[me], small_sem.at[5]))
+    for load in small + loads:
         load.start()
 
     def send(src, dst, phase, p):
@@ -74,17 +86,21 @@
         part = buf.at[pl.ds(0, n - 1)]
         pltpu.make_async_copy(part, part, sem).wait()
 
-    ext[0, EDGE:EDGE + lines, :] = displace[...]
-    ext[1, EDGE:EDGE + lines, :] = velocity[...]
-    ext[2, EDGE:EDGE + lines, :] = stiffness[...]
-    own = owners[...].astype(F32)
+    vd[nc + npast:cols] = jnp.zeros((cols - nc - npast, slots, 128), BF16)
+    gram[...] = jnp.zeros_like(gram)
+    prow[...] = jnp.zeros_like(prow)
+    small[0].wait()
+    same = iota((lines, lines), 0) == iota((lines, lines), 1)
+    own_row = jnp.broadcast_to(own_v[...].astype(F32), (lines, lines))
+    own = jnp.sum(jnp.where(same, own_row, 0.0), axis=1, keepdims=True)
     lane_f = iota((lines, 128), 1).astype(F32)
     onehot = jnp.where(own == lane_f, 1.0, 0.0)
     cnt[me] = jnp.broadcast_to(jnp.sum(onehot, axis=0, keepdims=True), (8, 128))
     if wide != per:
+        small[5].wait()
         stage[...] = jnp.zeros_like(stage)
         for s in range(n):
-            stage[s, 0:per, :] = press[s * per:(s + 1) * per, :]
+            stage[s, 0:per, :] = raw[s * per:(s + 1) * per, :]
 
     pl.semaphore_wait(barrier, n - 1)
     peers(lambda p: send(cnt.at[me], cnt.at[me], 0, p))
@@ -97,8 +113,6 @@
     peers(lambda p: send(press_block(p), pbuf.at[me], 1, p))
     if wide != per:
         pbuf[me] = stage[me]
-    else:
-        pbuf[me] = press[pl.ds(pl.multiple_of(me * per, 8), per), :]
 
     def halos(buf, first, lead):
         moves = []
@@ -114,6 +128,8 @@
             move.start()
         return moves
 
+    for load in small[1:4]:
+        load.wait()
     field_halo = halos(ext, 0, (slice(None),))
 
     below = jnp.where(iota((lines, lines), 0) > iota((lines, lines), 1), 1.0, 0.0).astype(BF16)
@@ -121,13 +137,8 @@
     rank = jnp.sum(earlier * onehot, axis=1, keepdims=True)
     slot = own * float(wide) + rank
     chooser = jnp.where(slot == iota((lines, total), 1).astype(F32), 1.0, 0.0).astype(BF16)
-    same = iota((lines, lines), 0) == iota((lines, lines), 1)
     slot_row = jnp.sum(jnp.where(same, slot, 0.0), axis=0, keepdims=True)
     placer = jnp.where(slot_row == iota((total, lines), 0).astype(F32), 1.0, 0.0).astype(BF16)
-
-    vd[nc + npast:cols] = jnp.zeros((cols - nc - npast, slots, 128), BF16)
-    gram[...] = jnp.zeros_like(gram)
-    prow[...] = jnp.zeros_like(prow)
 
     wait(cnt, recv_sem.at[0])
     mine = jnp.sum(jnp.where(iota((n, 8, 128), 2) == me, cnt[...], 0.0), axis=2, keepdims=True)
@@ -142,16 +153,10 @@
         return jnp.concatenate([cells[s, 0:per, :] for s in range(n)], axis=0)
 
     mask = compact(mask3)
-    mask_half = mask.astype(BF16)
+    halfmask[...] = mask.astype(BF16)
 
     loads[0].wait()
     loads[1].wait()
-
-    def apply_mask(k, carry):
-        vd[k] = vd[k] * mask_half
-        return carry
-
-    lax.fori_loop(0, nc + npast, apply_mask, 0)
 
     def gather(a):
         return jnp.concatenate([
@@ -159,8 +164,13 @@
             for r in range(slots // 16)], axis=1)
 
     def outer(a, carry):
+        for r in range(slots // 16):
+            rows16 = slice(r * 16, (r + 1) * 16)
+            block = vd[pl.ds(a * 16, 16), rows16, :] * halfmask[rows16, :][None]
+            masked[:, r * 128:(r + 1) * 128] = block.reshape(256, 128)
+
         def inner(b, carry):
-            prod = dot(gather(a), gather(b), ((1,), (1,)))
+            prod = dot(masked[...], gather(b), ((1,), (1,)))
             alike = (iota((256, 256), 0) & 15) == (iota((256, 256), 1) & 15)
             kept = jnp.where(alike, prod, 0.0).reshape(16, 16, 256)
             kept = jnp.sum(kept, axis=1) * jnp.where(a == b, 0.5, 1.0)
@@ -173,19 +183,17 @@
 
         return lax.fori_loop(a, cols // 16, inner, carry)
 
-    lax.fori_loop(0, cols // 16, outer, 0)
-    peers(lambda p: send(gram.at[p], rsbuf.at[me], 2, p))
-    rsbuf[me] = gram[me]
+    lax.fori_loop(0, 1, outer, 0)
 
     wait(pbuf, recv_sem.at[1])
+    if wide == per:
+        small[5].wait()
     returned = pbuf[...].reshape(total, 128)
     hi, mid, low = split3(returned)
     pext[EDGE:EDGE + lines, :] = dot(chooser, hi) + dot(chooser, mid) + dot(chooser, low)
     press_halo = halos(pext, 2, ())
 
-    wait(rsbuf, recv_sem.at[2])
-    agbuf[me] = jnp.sum(rsbuf[...], axis=0)
-    peers(lambda p: send(agbuf.at[me], agbuf.at[me], 3, p))
+    lax.fori_loop(1, 2, outer, 0)
 
     for move in field_halo:
         move.wait()
@@ -211,6 +219,31 @@
     field_ref[...] = field
     speed_ref[...] = v[EDGE:EDGE + lines, :]
 
+    lax.fori_loop(2, cols // 16, outer, 0)
+    peers(lambda p: send(gram.at[p], rsbuf.at[me], 2, p))
+    rsbuf[me] = gram[me]
+
+    wait(xbuf, recv_sem.at[4])
+    small[4].wait()
+    x_tilde = compact(xbuf[...])
+    resid = (mask * (x_tilde - iter_v[...])).astype(BF16).astype(F32)
+
+    def product(k, carry):
+        for u in range(10):
+            prow[pl.ds(k * 10 + u, 1), :] = jnp.sum(
+                vd[k * 10 + u].astype(F32) * resid, axis=0, keepdims=True)
+        return carry
+
+    lax.fori_loop(0, (nc + npast) // 10, product, 0)
+    ones = jnp.ones((8, 128), BF16)
+    hi, mid, low = split3(prow[...])
+    arbuf[me] = (dot(ones, hi, ((1,), (1,))) + dot(ones, mid, ((1,), (1,)))
+                 + dot(ones, low, ((1,), (1,))))
+    peers(lambda p: send(arbuf.at[me], arbuf.at[me], 5, p))
+    wait(rsbuf, recv_sem.at[2])
+    agbuf[me] = jnp.sum(rsbuf[...], axis=0)
+    peers(lambda p: send(agbuf.at[me], agbuf.at[me], 3, p))
+
     wait(agbuf, recv_sem.at[3])
     half = agbuf[0:16].reshape(128, 128)
     full = half + half.T
@@ -238,20 +271,6 @@
         inverse.append(jnp.where(lane2 < nc, pltpu.roll(done[part], 64, 1), 0.0))
         pivots.append(jnp.sum(jnp.where(diag2, done[part], 0.0), axis=1, keepdims=True))
 
-    wait(xbuf, recv_sem.at[4])
-    x_tilde = compact(xbuf[...])
-    resid = (mask * (x_tilde - iterate[...])).astype(BF16).astype(F32)
-
-    def product(k, carry):
-        prow[pl.ds(k, 1), :] = jnp.sum(vd[k].astype(F32) * resid, axis=0, keepdims=True)
-        return carry
-
-    lax.fori_loop(0, nc + npast, product, 0)
-    ones = jnp.ones((8, 128), BF16)
-    hi, mid, low = split3(prow[...])
-    arbuf[me] = (dot(ones, hi, ((1,), (1,))) + dot(ones, mid, ((1,), (1,)))
-                 + dot(ones, low, ((1,), (1,))))
-    peers(lambda p: send(arbuf.at[me], arbuf.at[me], 5, p))
     loads[2].wait()
     loads[3].wait()
     wait(arbuf, recv_sem.at[5])
@@ -271,13 +290,24 @@
             column, (nc, 128)).astype(BF16).astype(F32)
 
     def accumulate(k, acc):
-        return acc + coefs[pl.ds(k, 1), :] * vs[k].astype(F32)
-
-    update = lax.fori_loop(0, nc + npast, accumulate, jnp.zeros((slots, 128), F32))
+        for u in range(10):
+            acc = acc + coefs[pl.ds(k * 10 + u, 1), :] * vs[k * 10 + u].astype(F32)
+        return acc
+
+    update = lax.fori_loop(0, (nc + npast) // 10, accumulate, jnp.zeros((slots, 128), F32))
     new_ref[...] = mask * (x_tilde + update)
 
     for phase, buf in enumerate((cnt, pbuf, rsbuf, agbuf, xbuf, arbuf)):
         wait(buf, send_sem.at[phase])
+
+
+def hand_over(a, b, c, a_out, b_out, c_out, sems):
+    moves = [pltpu.make_async_copy(src, dst, sems.at[i])
+             for i, (src, dst) in enumerate(((a, a_out), (b, b_out), (c, c_out)))]
+    for move in moves:
+        move.start()
+    for move in moves:
+        move.wait()
 
 
 def local(press, iterate, displace, velocity, stiffness, owners, diff_cur, step_cur, diff_past, step_past):
@@ -291,21 +321,26 @@
     hbm = pl.BlockSpec(memory_space=pl.ANY)
     tiles = pltpu.VMEM((n, 8, 128), F32)
     blocks = pltpu.VMEM((n, wide, 128), F32)
-    return pl.pallas_call(
+    outs = pl.pallas_call(
         functools.partial(kernel, n, per, wide),
         out_shape=(
             jax.ShapeDtypeStruct((slots, 128), F32),
             jax.ShapeDtypeStruct((lines, 128), F32),
             jax.ShapeDtypeStruct((lines, 128), F32),
         ),
-        in_specs=[vmem] * 6 + [hbm] * 4,
+        in_specs=[hbm] * 10,
         out_specs=(vmem, vmem, vmem),
         scratch_shapes=[
             pltpu.VMEM((cols, slots, 128), BF16),
             pltpu.VMEM((nc + npast, slots, 128), BF16),
+            pltpu.VMEM((256, slots // 16 * 128), BF16),
+            pltpu.VMEM((slots, 128), BF16),
+            pltpu.VMEM((slots, 128), F32),
+            pltpu.VMEM((1, lines), jnp.int32),
             pltpu.VMEM((3, lines + 2 * EDGE, 128), F32),
             pltpu.VMEM((lines + 2 * EDGE, 128), F32),
             tiles,
+            pltpu.VMEM((slots if wide != per else 8, 128), F32),
             blocks if wide != per else pltpu.VMEM((8, 128), F32),
             blocks, blocks, blocks,
             tiles, tiles, tiles,
@@ -316,12 +351,22 @@
             pltpu.SemaphoreType.DMA((4,)),
             pltpu.SemaphoreType.DMA((6,)),
             pltpu.SemaphoreType.DMA((6,)),
+            pltpu.SemaphoreType.DMA((6,)),
             pltpu.SemaphoreType.DMA((4,)),
             pltpu.SemaphoreType.DMA((4,)),
         ],
         compiler_params=pltpu.CompilerParams(
-            collective_id=0, has_side_effects=True, vmem_limit_bytes=44 * 1024 * 1024),
-    )(press, iterate, displace, velocity, stiffness, owners, diff_cur, step_cur, diff_past, step_past)
+            collective_id=0, has_side_effects=True, vmem_limit_bytes=62 * 1024 * 1024),
+    )(press, iterate, displace, velocity, stiffness, owners.reshape(1, lines),
+      diff_cur, step_cur, diff_past, step_past)
+    return pl.pallas_call(
+        hand_over,
+        out_shape=tuple(jax.ShapeDtypeStruct(out.shape, out.dtype) for out in outs),
+        in_specs=[hbm] * 3,
+        out_specs=(hbm,) * 3,
+        scratch_shapes=[pltpu.SemaphoreType.DMA((3,))],
+        compiler_params=pltpu.CompilerParams(vmem_limit_bytes=62 * 1024 * 1024),
+    )(*outs)
 
 
 def solution(mesh):

time: 59.5 us -> 49.1 us (0.83)
  local copies, waits for them, and re-layouts: 13.6 us -> 0 us
  Pallas kernels: 44.9 us -> 48.3 us
    unnamed x22 -> x0, local copies, waits for them, and re-layouts: 13.6 us -> none
    pallas_call x0 -> x1, Pallas kernels: none -> 9.07 us  [local(): pl.pallas_call(hand_over, out_shape=tuple((jax.ShapeDtypeStruct(out.shape...]
    pallas_call x1, Pallas kernels: 44.9 us -> 39.2 us  [local(): pl.pallas_call(functools.partial(kernel, n, per, wide), out_shape=(jax.Sh...]
where the time goes in v2:
time: 49.1 us; the launch traced here: 48.9 us
  Pallas kernels  48.3 us (98%)
  between operations  0.64 us (1%)
    pallas_call x1, Pallas kernels, local(): pl.pallas_call(functools.partial(kernel, n, per, wide), out_shape=(jax.Sh...  39.2 us
    pallas_call x1, Pallas kernels, local(): pl.pallas_call(hand_over, out_shape=tuple((jax.ShapeDtypeStruct(out.shape...  9.07 us

profile of v2, /device:TPU:0, one launch (start us, length us, event | category | flops | bytes accessed | tf_op | source)
XLA Modules:
  0.0 48.9 jit_solution(16335286173781587780)
XLA Ops:
  0.6 39.2 %shard_map.121 = (f32[256,128]{1,0:T(8,128)}, f32[128,128]{1,0:T(8,128)}, f32[128,128]{1,0:T(8,128)}) custom-call(f32[256,128]{1,0:T(8,128)} %press.1, f32[256,128]{1,0:T(8,128)} %iterate.1, f32[128,128]{1,0:T(8,128)} %displace.1, f32[128,128]{1,0:T(8,128)} %velocity.1, f32[128,128]{1,0:T(8,128)} %stiffness.1, s32[1,128]{1,0:T(1,128)} %bitcast.1, ...), custom_call_target="tpu_custom_call" | custom-call | tf_op jit(solution)/shard_map/pallas_call | solution.py:324
  39.8 9.1 %shard_map.122 = (f32[256,128]{1,0:T(8,128)}, f32[128,128]{1,0:T(8,128)}, f32[128,128]{1,0:T(8,128)}) custom-call(f32[256,128]{1,0:T(8,128)} %get-tuple-element.6.a, f32[128,128]{1,0:T(8,128)} %get-tuple-element.7.b, f32[128,128]{1,0:T(8,128)} %get-tuple-element.8.c), custom_call_target="tpu_custom_call" | custom-call | tf_op jit(solution)/shard_map/pallas_call | solution.py:362

commit v3 on v2

--- a/solution.py
+++ b/solution.py
@@ -34,7 +34,7 @@
     n, per, wide,
     press, iterate, displace, velocity, stiffness, owners, diff_cur, step_cur, diff_past, step_past,
     new_ref, field_ref, speed_ref,
-    vd, vs, masked, halfmask, iter_v, own_v, ext, pext, cnt, raw, stage, pbuf, obuf, xbuf, gram, rsbuf, agbuf, prow, arbuf, elim, coefs,
+    vd, vs, masked, kbuf, halfmask, iter_v, own_v, ext, pext, cnt, raw, stage, pbuf, obuf, xbuf, gram, rsbuf, agbuf, prow, arbuf, elim, coefs,
     load_sem, small_sem, send_sem, recv_sem, halo_send, halo_recv,
 ):
     me = lax.axis_index("tile")
@@ -88,6 +88,7 @@
 
     vd[nc + npast:cols] = jnp.zeros((cols - nc - npast, slots, 128), BF16)
     gram[...] = jnp.zeros_like(gram)
+    kbuf[...] = jnp.zeros_like(kbuf)
     prow[...] = jnp.zeros_like(prow)
     small[0].wait()
     same = iota((lines, lines), 0) == iota((lines, lines), 1)
@@ -174,11 +175,7 @@
             alike = (iota((256, 256), 0) & 15) == (iota((256, 256), 1) & 15)
             kept = jnp.where(alike, prod, 0.0).reshape(16, 16, 256)
             kept = jnp.sum(kept, axis=1) * jnp.where(a == b, 0.5, 1.0)
-            spread = jnp.where((iota((256, 128), 0) >> 4) + b * 16 == iota((256, 128), 1), 1.0, 0.0)
-            spread = spread.astype(BF16)
-            hi, mid, low = split3(kept)
-            value = dot(hi, spread) + dot(mid, spread) + dot(low, spread)
-            gram[pl.ds(2 * a, 2)] += value.reshape(2, 8, 128)
+            kbuf[pl.ds(pl.multiple_of(a * 16, 16), 16), pl.ds(pl.multiple_of(b * 256, 256), 256)] = kept
             return carry
 
         return lax.fori_loop(a, cols // 16, inner, carry)
@@ -220,6 +217,11 @@
     speed_ref[...] = v[EDGE:EDGE + lines, :]
 
     lax.fori_loop(2, cols // 16, outer, 0)
+    spread = jnp.where((iota((cols * 16, 128), 0) >> 4) == iota((cols * 16, 128), 1), 1.0, 0.0)
+    spread = spread.astype(BF16)
+    hi, mid, low = split3(kbuf[...])
+    value = dot(hi, spread) + dot(mid, spread) + dot(low, spread)
+    gram[0:cols // 8] = value.reshape(cols // 8, 8, 128)
     peers(lambda p: send(gram.at[p], rsbuf.at[me], 2, p))
     rsbuf[me] = gram[me]
 
@@ -255,15 +257,26 @@
     elim[1] = past_part + unit + jnp.where((lane2 == sub2) & (sub2 >= npast), 1.0, 0.0)
     lane3, sub3 = iota((2, nc, 128), 2), iota((2, nc, 128), 1)
 
-    def eliminate(j, carry):
+    lane1 = iota((2, 1, 128), 2)
+
+    def eliminate(i, carry):
+        j = 2 * i
         now = elim[...]
-        row = elim[:, pl.ds(j, 1), :]
-        col = jnp.sum(jnp.where(lane3 == j, now, 0.0), axis=2, keepdims=True)
-        pivot = jnp.sum(jnp.where(iota((2, 1, 128), 2) == j, row, 0.0), axis=2, keepdims=True)
-        elim[...] = jnp.where(sub3 > j, now - col * (row / pivot), now)
+        row0, row1 = elim[:, pl.ds(j, 1), :], elim[:, pl.ds(j + 1, 1), :]
+        col0 = jnp.sum(jnp.where(lane3 == j, now, 0.0), axis=2, keepdims=True)
+        col1 = jnp.sum(jnp.where(lane3 == j + 1, now, 0.0), axis=2, keepdims=True)
+        top = jnp.sum(jnp.where(lane1 == j, row0, 0.0), axis=2, keepdims=True)
+        side = jnp.sum(jnp.where(lane1 == j, row1, 0.0), axis=2, keepdims=True)
+        corner = jnp.sum(jnp.where(lane1 == j + 1, row1, 0.0), axis=2, keepdims=True)
+        factor = side / top
+        row1 = row1 - factor * row0
+        col1 = col1 - factor * col0
+        corner = corner - factor * side
+        later = now - col0 * (row0 / top) - col1 * (row1 / corner)
+        elim[...] = jnp.where(sub3 > j + 1, later, jnp.where(sub3 == j + 1, row1, now))
         return carry
 
-    lax.fori_loop(0, nc, eliminate, 0)
+    lax.fori_loop(0, nc // 2, eliminate, 0)
     done = elim[...]
     diag2 = lane2 == sub2
     inverse, pivots = [], []
@@ -301,12 +314,16 @@
         wait(buf, send_sem.at[phase])
 
 
-def hand_over(a, b, c, a_out, b_out, c_out, sems):
-    moves = [pltpu.make_async_copy(src, dst, sems.at[i])
-             for i, (src, dst) in enumerate(((a, a_out), (b, b_out), (c, c_out)))]
-    for move in moves:
+def hand_over(a, b, c, a_out, b_out, c_out, a_held, b_held, c_held, sems):
+    pairs = ((a, a_held, a_out), (b, b_held, b_out), (c, c_held, c_out))
+    fetch = [pltpu.make_async_copy(src, held, sems.at[0, i]) for i, (src, held, _) in enumerate(pairs)]
+    store = [pltpu.make_async_copy(held, dst, sems.at[1, i]) for i, (_, held, dst) in enumerate(pairs)]
+    for move in fetch:
         move.start()
-    for move in moves:
+    for move, after in zip(fetch, store):
+        move.wait()
+        after.start()
+    for move in store:
         move.wait()
 
 
@@ -334,6 +351,7 @@
             pltpu.VMEM((cols, slots, 128), BF16),
             pltpu.VMEM((nc + npast, slots, 128), BF16),
             pltpu.VMEM((256, slots // 16 * 128), BF16),
+            pltpu.VMEM((cols, cols * 16), F32),
             pltpu.VMEM((slots, 128), BF16),
             pltpu.VMEM((slots, 128), F32),
             pltpu.VMEM((1, lines), jnp.int32),
@@ -364,7 +382,8 @@
         out_shape=tuple(jax.ShapeDtypeStruct(out.shape, out.dtype) for out in outs),
         in_specs=[hbm] * 3,
         out_specs=(hbm,) * 3,
-        scratch_shapes=[pltpu.SemaphoreType.DMA((3,))],
+        scratch_shapes=[pltpu.VMEM(out.shape, out.dtype) for out in outs]
+        + [pltpu.SemaphoreType.DMA((2, 3))],
         compiler_params=pltpu.CompilerParams(vmem_limit_bytes=62 * 1024 * 1024),
     )(*outs)
 

time: 49.1 us -> 38 us (0.77)
  Pallas kernels: 48.3 us -> 37.2 us
    pallas_call x1, Pallas kernels: 9.07 us -> 1.65 us  [local(): pl.pallas_call(hand_over, out_shape=tuple((jax.ShapeDtypeStruct(out.shape...]
    pallas_call x1, Pallas kernels: 39.2 us -> 35.5 us  [local(): pl.pallas_call(functools.partial(kernel, n, per, wide), out_shape=(jax.Sh...]
where the time goes in v3:
time: 38 us; the launch traced here: 37.8 us
  Pallas kernels  37.2 us (98%)
  between operations  0.64 us (2%)
    pallas_call x1, Pallas kernels, local(): pl.pallas_call(functools.partial(kernel, n, per, wide), out_shape=(jax.Sh...  35.5 us
    pallas_call x1, Pallas kernels, local(): pl.pallas_call(hand_over, out_shape=tuple((jax.ShapeDtypeStruct(out.shape...  1.65 us

profile of v3, /device:TPU:0, one launch (start us, length us, event | category | flops | bytes accessed | tf_op | source)
XLA Modules:
  0.0 37.8 jit_solution(10315774301675500842)
XLA Ops:
  0.6 35.5 %shard_map.121 = (f32[256,128]{1,0:T(8,128)}, f32[128,128]{1,0:T(8,128)}, f32[128,128]{1,0:T(8,128)}) custom-call(f32[256,128]{1,0:T(8,128)} %press.1, f32[256,128]{1,0:T(8,128)} %iterate.1, f32[128,128]{1,0:T(8,128)} %displace.1, f32[128,128]{1,0:T(8,128)} %velocity.1, f32[128,128]{1,0:T(8,128)} %stiffness.1, s32[1,128]{1,0:T(1,128)} %bitcast.1, ...), custom_call_target="tpu_custom_call" | custom-call | tf_op jit(solution)/shard_map/pallas_call | solution.py:341
  36.2 1.7 %shard_map.122 = (f32[256,128]{1,0:T(8,128)}, f32[128,128]{1,0:T(8,128)}, f32[128,128]{1,0:T(8,128)}) custom-call(f32[256,128]{1,0:T(8,128)} %get-tuple-element.6.a, f32[128,128]{1,0:T(8,128)} %get-tuple-element.7.b, f32[128,128]{1,0:T(8,128)} %get-tuple-element.8.c), custom_call_target="tpu_custom_call" | custom-call | tf_op jit(solution)/shard_map/pallas_call | solution.py:380

commit v4 on v3

--- a/solution.py
+++ b/solution.py
@@ -161,26 +161,22 @@
 
     def gather(a):
         return jnp.concatenate([
-            vd[pl.ds(a * 16, 16), r * 16:(r + 1) * 16, :].reshape(256, 128)
+            vd[a * 16:(a + 1) * 16, r * 16:(r + 1) * 16, :].reshape(256, 128)
             for r in range(slots // 16)], axis=1)
 
-    def outer(a, carry):
+    alike = (iota((256, 256), 0) & 15) == (iota((256, 256), 1) & 15)
+
+    def gram_rows(a):
         for r in range(slots // 16):
             rows16 = slice(r * 16, (r + 1) * 16)
-            block = vd[pl.ds(a * 16, 16), rows16, :] * halfmask[rows16, :][None]
-            masked[:, r * 128:(r + 1) * 128] = block.reshape(256, 128)
-
-        def inner(b, carry):
-            prod = dot(masked[...], gather(b), ((1,), (1,)))
-            alike = (iota((256, 256), 0) & 15) == (iota((256, 256), 1) & 15)
-            kept = jnp.where(alike, prod, 0.0).reshape(16, 16, 256)
-            kept = jnp.sum(kept, axis=1) * jnp.where(a == b, 0.5, 1.0)
-            kbuf[pl.ds(pl.multiple_of(a * 16, 16), 16), pl.ds(pl.multiple_of(b * 256, 256), 256)] = kept
-            return carry
-
-        return lax.fori_loop(a, cols // 16, inner, carry)
-
-    lax.fori_loop(0, 1, outer, 0)
+            block = vd[a * 16:(a + 1) * 16, rows16, :] * halfmask[rows16, :][None]
+            masked[a % 2, :, r * 128:(r + 1) * 128] = block.reshape(256, 128)
+        for b in range(a, cols // 16):
+            prod = dot(masked[a % 2], gather(b), ((1,), (1,)))
+            kept = jnp.sum(jnp.where(alike, prod, 0.0).reshape(16, 16, 256), axis=1)
+            kbuf[a * 16:(a + 1) * 16, b * 256:(b + 1) * 256] = 0.5 * kept if a == b else kept
+
+    gram_rows(0)
 
     wait(pbuf, recv_sem.at[1])
     if wide == per:
@@ -190,7 +186,7 @@
     pext[EDGE:EDGE + lines, :] = dot(chooser, hi) + dot(chooser, mid) + dot(chooser, low)
     press_halo = halos(pext, 2, ())
 
-    lax.fori_loop(1, 2, outer, 0)
+    gram_rows(1)
 
     for move in field_halo:
         move.wait()
@@ -216,7 +212,8 @@
     field_ref[...] = field
     speed_ref[...] = v[EDGE:EDGE + lines, :]
 
-    lax.fori_loop(2, cols // 16, outer, 0)
+    for a in range(2, cols // 16):
+        gram_rows(a)
     spread = jnp.where((iota((cols * 16, 128), 0) >> 4) == iota((cols * 16, 128), 1), 1.0, 0.0)
     spread = spread.astype(BF16)
     hi, mid, low = split3(kbuf[...])
@@ -236,15 +233,19 @@
                 vd[k * 10 + u].astype(F32) * resid, axis=0, keepdims=True)
         return carry
 
-    lax.fori_loop(0, (nc + npast) // 10, product, 0)
+    steps = (nc + npast) // 10
+    lax.fori_loop(0, steps // 2, product, 0)
+
+    wait(rsbuf, recv_sem.at[2])
+    agbuf[me] = jnp.sum(rsbuf[...], axis=0)
+    peers(lambda p: send(agbuf.at[me], agbuf.at[me], 3, p))
+
+    lax.fori_loop(steps // 2, steps, product, 0)
     ones = jnp.ones((8, 128), BF16)
     hi, mid, low = split3(prow[...])
     arbuf[me] = (dot(ones, hi, ((1,), (1,))) + dot(ones, mid, ((1,), (1,)))
                  + dot(ones, low, ((1,), (1,))))
     peers(lambda p: send(arbuf.at[me], arbuf.at[me], 5, p))
-    wait(rsbuf, recv_sem.at[2])
-    agbuf[me] = jnp.sum(rsbuf[...], axis=0)
-    peers(lambda p: send(agbuf.at[me], agbuf.at[me], 3, p))
 
     wait(agbuf, recv_sem.at[3])
     half = agbuf[0:16].reshape(128, 128)
@@ -350,7 +351,7 @@
         scratch_shapes=[
             pltpu.VMEM((cols, slots, 128), BF16),
             pltpu.VMEM((nc + npast, slots, 128), BF16),
-            pltpu.VMEM((256, slots // 16 * 128), BF16),
+            pltpu.VMEM((2, 256, slots // 16 * 128), BF16),
             pltpu.VMEM((cols, cols * 16), F32),
             pltpu.VMEM((slots, 128), BF16),
             pltpu.VMEM((slots, 128), F32),

time: 38 us -> 35.4 us (0.932)
  Pallas kernels: 37.2 us -> 34.6 us
    pallas_call x1, Pallas kernels: 35.5 us -> 32.9 us  [local(): pl.pallas_call(functools.partial(kernel, n, per, wide), out_shape=(jax.Sh...]
where the time goes in v4:
time: 35.4 us; the launch traced here: 35.2 us
  Pallas kernels  34.6 us (98%)
  between operations  0.64 us (2%)
    pallas_call x1, Pallas kernels, local(): pl.pallas_call(functools.partial(kernel, n, per, wide), out_shape=(jax.Sh...  32.9 us
    pallas_call x1, Pallas kernels, local(): pl.pallas_call(hand_over, out_shape=tuple((jax.ShapeDtypeStruct(out.shape...  1.65 us

profile of v4, /device:TPU:0, one launch (start us, length us, event | category | flops | bytes accessed | tf_op | source)
XLA Modules:
  0.0 35.2 jit_solution(7201484860142140004)
XLA Ops:
  0.6 32.9 %shard_map.121 = (f32[256,128]{1,0:T(8,128)}, f32[128,128]{1,0:T(8,128)}, f32[128,128]{1,0:T(8,128)}) custom-call(f32[256,128]{1,0:T(8,128)} %press.1, f32[256,128]{1,0:T(8,128)} %iterate.1, f32[128,128]{1,0:T(8,128)} %displace.1, f32[128,128]{1,0:T(8,128)} %velocity.1, f32[128,128]{1,0:T(8,128)} %stiffness.1, s32[1,128]{1,0:T(1,128)} %bitcast.1, ...), custom_call_target="tpu_custom_call" | custom-call | tf_op jit(solution)/shard_map/pallas_call | solution.py:342
  33.5 1.7 %shard_map.122 = (f32[256,128]{1,0:T(8,128)}, f32[128,128]{1,0:T(8,128)}, f32[128,128]{1,0:T(8,128)}) custom-call(f32[256,128]{1,0:T(8,128)} %get-tuple-element.6.a, f32[128,128]{1,0:T(8,128)} %get-tuple-element.7.b, f32[128,128]{1,0:T(8,128)} %get-tuple-element.8.c), custom_call_target="tpu_custom_call" | custom-call | tf_op jit(solution)/shard_map/pallas_call | solution.py:381

commit v5 on v4

--- a/solution.py
+++ b/solution.py
@@ -46,11 +46,14 @@
     total = n * wide
 
     def peers(fn):
+        group = next(g for g in (5, 3, 1) if (n - 1) % g == 0)
+
         def step(i, carry):
-            fn(lax.rem(me + i, n))
+            for u in range(group):
+                fn(lax.rem(me + (i * group + u + 1), n))
             return carry
 
-        lax.fori_loop(1, n, step, 0)
+        lax.fori_loop(0, (n - 1) // group, step, 0)
 
     barrier = pltpu.get_barrier_semaphore()
     peers(lambda p: pl.semaphore_signal(
@@ -260,24 +263,34 @@
 
     lane1 = iota((2, 1, 128), 2)
 
+    width = next(g for g in (4, 2, 1) if nc % g == 0)
+
+    def lane_of(cells, lanes, j):
+        return jnp.sum(jnp.where(lanes == j, cells, 0.0), axis=2, keepdims=True)
+
     def eliminate(i, carry):
-        j = 2 * i
+        j = width * i
         now = elim[...]
-        row0, row1 = elim[:, pl.ds(j, 1), :], elim[:, pl.ds(j + 1, 1), :]
-        col0 = jnp.sum(jnp.where(lane3 == j, now, 0.0), axis=2, keepdims=True)
-        col1 = jnp.sum(jnp.where(lane3 == j + 1, now, 0.0), axis=2, keepdims=True)
-        top = jnp.sum(jnp.where(lane1 == j, row0, 0.0), axis=2, keepdims=True)
-        side = jnp.sum(jnp.where(lane1 == j, row1, 0.0), axis=2, keepdims=True)
-        corner = jnp.sum(jnp.where(lane1 == j + 1, row1, 0.0), axis=2, keepdims=True)
-        factor = side / top
-        row1 = row1 - factor * row0
-        col1 = col1 - factor * col0
-        corner = corner - factor * side
-        later = now - col0 * (row0 / top) - col1 * (row1 / corner)
-        elim[...] = jnp.where(sub3 > j + 1, later, jnp.where(sub3 == j + 1, row1, now))
+        rows = [elim[:, pl.ds(j + u, 1), :] for u in range(width)]
+        columns = [lane_of(now, lane3, j + u) for u in range(width)]
+        entry = [[lane_of(rows[u], lane1, j + m) for m in range(u + 1)] for u in range(width)]
+        for m in range(width):
+            for u in range(m + 1, width):
+                factor = entry[u][m] / entry[m][m]
+                rows[u] = rows[u] - factor * rows[m]
+                columns[u] = columns[u] - factor * columns[m]
+                for k in range(m + 1, u + 1):
+                    entry[u][k] = entry[u][k] - factor * entry[k][m]
+        later = now
+        for u in range(width):
+            later = later - columns[u] * (rows[u] / entry[u][u])
+        result = jnp.where(sub3 >= j + width, later, now)
+        for u in range(1, width):
+            result = jnp.where(sub3 == j + u, rows[u], result)
+        elim[...] = result
         return carry
 
-    lax.fori_loop(0, nc // 2, eliminate, 0)
+    lax.fori_loop(0, nc // width, eliminate, 0)
     done = elim[...]
     diag2 = lane2 == sub2
     inverse, pivots = [], []

time: 35.4 us -> 34.6 us (0.977)
  Pallas kernels: 34.6 us -> 33.8 us
    pallas_call x1, Pallas kernels: 32.9 us -> 32.1 us  [local(): pl.pallas_call(functools.partial(kernel, n, per, wide), out_shape=(jax.Sh...]
where the time goes in v5:
time: 34.6 us; the launch traced here: 34.4 us
  Pallas kernels  33.8 us (98%)
  between operations  0.64 us (2%)
    pallas_call x1, Pallas kernels, local(): pl.pallas_call(functools.partial(kernel, n, per, wide), out_shape=(jax.Sh...  32.1 us
    pallas_call x1, Pallas kernels, local(): pl.pallas_call(hand_over, out_shape=tuple((jax.ShapeDtypeStruct(out.shape...  1.65 us

profile of v5, /device:TPU:0, one launch (start us, length us, event | category | flops | bytes accessed | tf_op | source)
XLA Modules:
  0.0 34.4 jit_solution(5030818947101689904)
XLA Ops:
  0.6 32.1 %shard_map.121 = (f32[256,128]{1,0:T(8,128)}, f32[128,128]{1,0:T(8,128)}, f32[128,128]{1,0:T(8,128)}) custom-call(f32[256,128]{1,0:T(8,128)} %press.1, f32[256,128]{1,0:T(8,128)} %iterate.1, f32[128,128]{1,0:T(8,128)} %displace.1, f32[128,128]{1,0:T(8,128)} %velocity.1, f32[128,128]{1,0:T(8,128)} %stiffness.1, s32[1,128]{1,0:T(1,128)} %bitcast.1, ...), custom_call_target="tpu_custom_call" | custom-call | tf_op jit(solution)/shard_map/pallas_call | solution.py:355
  32.8 1.7 %shard_map.122 = (f32[256,128]{1,0:T(8,128)}, f32[128,128]{1,0:T(8,128)}, f32[128,128]{1,0:T(8,128)}) custom-call(f32[256,128]{1,0:T(8,128)} %get-tuple-element.6.a, f32[128,128]{1,0:T(8,128)} %get-tuple-element.7.b, f32[128,128]{1,0:T(8,128)} %get-tuple-element.8.c), custom_call_target="tpu_custom_call" | custom-call | tf_op jit(solution)/shard_map/pallas_call | solution.py:394

commit v6 on v5

--- a/solution.py
+++ b/solution.py
@@ -42,7 +42,7 @@
     lines = displace.shape[0]
     slots = iterate.shape[0]
     nc, npast = diff_cur.shape[0], diff_past.shape[0]
-    cols = vd.shape[0]
+    cols = kbuf.shape[0]
     total = n * wide
 
     def peers(fn):
@@ -89,7 +89,7 @@
         part = buf.at[pl.ds(0, n - 1)]
         pltpu.make_async_copy(part, part, sem).wait()
 
-    vd[nc + npast:cols] = jnp.zeros((cols - nc - npast, slots, 128), BF16)
+    vd[nc + npast:] = jnp.zeros((vd.shape[0] - nc - npast, slots, 128), BF16)
     gram[...] = jnp.zeros_like(gram)
     kbuf[...] = jnp.zeros_like(kbuf)
     prow[...] = jnp.zeros_like(prow)
@@ -162,22 +162,29 @@
     loads[0].wait()
     loads[1].wait()
 
+    used = vd.shape[0]
+    sizes = [min(16, used - a * 16) for a in range(cols // 16)]
+
     def gather(a):
+        size = sizes[a]
         return jnp.concatenate([
-            vd[a * 16:(a + 1) * 16, r * 16:(r + 1) * 16, :].reshape(256, 128)
+            vd[a * 16:a * 16 + size, r * 16:(r + 1) * 16, :].reshape(size * 16, 128)
             for r in range(slots // 16)], axis=1)
 
     alike = (iota((256, 256), 0) & 15) == (iota((256, 256), 1) & 15)
 
     def gram_rows(a):
+        size = sizes[a]
         for r in range(slots // 16):
             rows16 = slice(r * 16, (r + 1) * 16)
-            block = vd[a * 16:(a + 1) * 16, rows16, :] * halfmask[rows16, :][None]
-            masked[a % 2, :, r * 128:(r + 1) * 128] = block.reshape(256, 128)
+            block = vd[a * 16:a * 16 + size, rows16, :] * halfmask[rows16, :][None]
+            masked[a % 2, 0:size * 16, r * 128:(r + 1) * 128] = block.reshape(size * 16, 128)
         for b in range(a, cols // 16):
-            prod = dot(masked[a % 2], gather(b), ((1,), (1,)))
-            kept = jnp.sum(jnp.where(alike, prod, 0.0).reshape(16, 16, 256), axis=1)
-            kbuf[a * 16:(a + 1) * 16, b * 256:(b + 1) * 256] = 0.5 * kept if a == b else kept
+            high, wide_b = size * 16, sizes[b] * 16
+            prod = dot(masked[a % 2, 0:high, :], gather(b), ((1,), (1,)))
+            kept = jnp.where(alike[0:high, 0:wide_b], prod, 0.0).reshape(size, 16, wide_b)
+            kept = jnp.sum(kept, axis=1)
+            kbuf[a * 16:a * 16 + size, b * 256:b * 256 + wide_b] = 0.5 * kept if a == b else kept
 
     gram_rows(0)
 
@@ -268,10 +275,8 @@
     def lane_of(cells, lanes, j):
         return jnp.sum(jnp.where(lanes == j, cells, 0.0), axis=2, keepdims=True)
 
-    def eliminate(i, carry):
-        j = width * i
-        now = elim[...]
-        rows = [elim[:, pl.ds(j + u, 1), :] for u in range(width)]
+    def eliminate(j, now):
+        rows = [now[:, j + u:j + u + 1, :] for u in range(width)]
         columns = [lane_of(now, lane3, j + u) for u in range(width)]
         entry = [[lane_of(rows[u], lane1, j + m) for m in range(u + 1)] for u in range(width)]
         for m in range(width):
@@ -287,11 +292,11 @@
         result = jnp.where(sub3 >= j + width, later, now)
         for u in range(1, width):
             result = jnp.where(sub3 == j + u, rows[u], result)
-        elim[...] = result
-        return carry
-
-    lax.fori_loop(0, nc // width, eliminate, 0)
+        return result
+
     done = elim[...]
+    for j in range(0, nc, width):
+        done = eliminate(j, done)
     diag2 = lane2 == sub2
     inverse, pivots = [], []
     for part in range(2):
@@ -362,7 +367,7 @@
         in_specs=[hbm] * 10,
         out_specs=(vmem, vmem, vmem),
         scratch_shapes=[
-            pltpu.VMEM((cols, slots, 128), BF16),
+            pltpu.VMEM((-(-(nc + npast) // 8) * 8, slots, 128), BF16),
             pltpu.VMEM((nc + npast, slots, 128), BF16),
             pltpu.VMEM((2, 256, slots // 16 * 128), BF16),
             pltpu.VMEM((cols, cols * 16), F32),

time: 34.6 us -> 35.4 us (1.023)
  Pallas kernels: 33.8 us -> 34.6 us
    pallas_call x1, Pallas kernels: 32.1 us -> 32.9 us  [local(): pl.pallas_call(functools.partial(kernel, n, per, wide), out_shape=(jax.Sh...]
where the time goes in v6:
time: 35.4 us; the launch traced here: 35.2 us
  Pallas kernels  34.6 us (98%)
  between operations  0.64 us (2%)
    pallas_call x1, Pallas kernels, local(): pl.pallas_call(functools.partial(kernel, n, per, wide), out_shape=(jax.Sh...  32.9 us
    pallas_call x1, Pallas kernels, local(): pl.pallas_call(hand_over, out_shape=tuple((jax.ShapeDtypeStruct(out.shape...  1.65 us

profile of v6, /device:TPU:0, one launch (start us, length us, event | category | flops | bytes accessed | tf_op | source)
XLA Modules:
  0.0 35.2 jit_solution(5857573543325410918)
XLA Ops:
  0.6 32.9 %shard_map.121 = (f32[256,128]{1,0:T(8,128)}, f32[128,128]{1,0:T(8,128)}, f32[128,128]{1,0:T(8,128)}) custom-call(f32[256,128]{1,0:T(8,128)} %press.1, f32[256,128]{1,0:T(8,128)} %iterate.1, f32[128,128]{1,0:T(8,128)} %displace.1, f32[128,128]{1,0:T(8,128)} %velocity.1, f32[128,128]{1,0:T(8,128)} %stiffness.1, s32[1,128]{1,0:T(1,128)} %bitcast.1, ...), custom_call_target="tpu_custom_call" | custom-call | tf_op jit(solution)/shard_map/pallas_call | solution.py:360
  33.6 1.7 %shard_map.122 = (f32[256,128]{1,0:T(8,128)}, f32[128,128]{1,0:T(8,128)}, f32[128,128]{1,0:T(8,128)}) custom-call(f32[256,128]{1,0:T(8,128)} %get-tuple-element.6.a, f32[128,128]{1,0:T(8,128)} %get-tuple-element.7.b, f32[128,128]{1,0:T(8,128)} %get-tuple-element.8.c), custom_call_target="tpu_custom_call" | custom-call | tf_op jit(solution)/shard_map/pallas_call | solution.py:399

commit v7 on v6

--- a/solution.py
+++ b/solution.py
@@ -275,8 +275,10 @@
     def lane_of(cells, lanes, j):
         return jnp.sum(jnp.where(lanes == j, cells, 0.0), axis=2, keepdims=True)
 
-    def eliminate(j, now):
-        rows = [now[:, j + u:j + u + 1, :] for u in range(width)]
+    def eliminate(i, carry):
+        j = width * i
+        now = elim[...]
+        rows = [elim[:, pl.ds(j + u, 1), :] for u in range(width)]
         columns = [lane_of(now, lane3, j + u) for u in range(width)]
         entry = [[lane_of(rows[u], lane1, j + m) for m in range(u + 1)] for u in range(width)]
         for m in range(width):
@@ -292,11 +294,11 @@
         result = jnp.where(sub3 >= j + width, later, now)
         for u in range(1, width):
             result = jnp.where(sub3 == j + u, rows[u], result)
-        return result
-
+        elim[...] = result
+        return carry
+
+    lax.fori_loop(0, nc // width, eliminate, 0)
     done = elim[...]
-    for j in range(0, nc, width):
-        done = eliminate(j, done)
     diag2 = lane2 == sub2
     inverse, pivots = [], []
     for part in range(2):

time: 35.4 us -> 34.4 us (0.972)
  Pallas kernels: 34.6 us -> 33.6 us
    pallas_call x1, Pallas kernels: 32.9 us -> 31.9 us  [local(): pl.pallas_call(functools.partial(kernel, n, per, wide), out_shape=(jax.Sh...]
where the time goes in v7:
time: 34.4 us; the launch traced here: 34.2 us
  Pallas kernels  33.6 us (98%)
  between operations  0.64 us (2%)
    pallas_call x1, Pallas kernels, local(): pl.pallas_call(functools.partial(kernel, n, per, wide), out_shape=(jax.Sh...  31.9 us
    pallas_call x1, Pallas kernels, local(): pl.pallas_call(hand_over, out_shape=tuple((jax.ShapeDtypeStruct(out.shape...  1.65 us

profile of v7, /device:TPU:0, one launch (start us, length us, event | category | flops | bytes accessed | tf_op | source)
XLA Modules:
  0.0 34.2 jit_solution(8748136848517812489)
XLA Ops:
  0.6 31.9 %shard_map.121 = (f32[256,128]{1,0:T(8,128)}, f32[128,128]{1,0:T(8,128)}, f32[128,128]{1,0:T(8,128)}) custom-call(f32[256,128]{1,0:T(8,128)} %press.1, f32[256,128]{1,0:T(8,128)} %iterate.1, f32[128,128]{1,0:T(8,128)} %displace.1, f32[128,128]{1,0:T(8,128)} %velocity.1, f32[128,128]{1,0:T(8,128)} %stiffness.1, s32[1,128]{1,0:T(1,128)} %bitcast.1, ...), custom_call_target="tpu_custom_call" | custom-call | tf_op jit(solution)/shard_map/pallas_call | solution.py:362
  32.6 1.7 %shard_map.122 = (f32[256,128]{1,0:T(8,128)}, f32[128,128]{1,0:T(8,128)}, f32[128,128]{1,0:T(8,128)}) custom-call(f32[256,128]{1,0:T(8,128)} %get-tuple-element.6.a, f32[128,128]{1,0:T(8,128)} %get-tuple-element.7.b, f32[128,128]{1,0:T(8,128)} %get-tuple-element.8.c), custom_call_target="tpu_custom_call" | custom-call | tf_op jit(solution)/shard_map/pallas_call | solution.py:401
